TPU v7x, 512 devices: a whole 4x8x8 slice. The times are simulated.
512 devices in a mesh: grp: 8 (over x, z_lo), col: 64 (over y, z_hi, core).
Axes of the slice: x: 4, y: 8, z: 8 (z_hi: 4, z_lo: 2; z = z_hi * 2 + z_lo), core: 2. Of those that a mesh axis runs over, the one named last changes fastest.
Arguments:
- out_grads: bfloat16 [1024, 28672], P('col', 'grp'), may hold values from -1.5 to 1.5
- in_acts: bfloat16 [1024, 8192], P(None, 'col'), may hold values from -1.5 to 1.5
- basis_out: bfloat16 [28672, 24576], P('grp', 'col'), may hold values from -0.03125 to 0.03125
- basis_in: bfloat16 [8192, 8192], P('col', 'grp'), may hold values from -0.0625 to 0.0625
Outputs:
- eigen_fit: float32 [24576, 8192], P('col', 'grp')
All inputs are finite; a program needn't handle non-finite values.
Results may differ from a plain program's by a relative error of at most 0.0034.
Values may be sent and summed in bfloat16 or wider, within the bound.
No kernel may reach another device: no remote copies, remote signals or barrier semaphores. Data moves between devices by JAX's collectives and lax.ppermute only.
A program may use at most 64 MiB of HBM per device.

v0:
```python
import jax
import jax.numpy as jnp
from jax import lax
from jax.sharding import PartitionSpec as P

T_SIZE = 256
SEQS = 4


def local(out_grads, in_acts, basis_out, basis_in):
    grad_partial = jnp.dot(
        lax.all_gather(out_grads, "col", axis=0, tiled=True),
        basis_out,
        preferred_element_type=jnp.float32,
    )
    grad_proj = lax.psum(grad_partial, "grp").astype(jnp.bfloat16)
    act_partial = jnp.dot(in_acts, basis_in, preferred_element_type=jnp.float32)
    act_proj = lax.psum(act_partial, "col").astype(jnp.bfloat16)
    grad_seq = grad_proj.reshape(SEQS, T_SIZE, grad_proj.shape[1])
    act_seq = act_proj.reshape(SEQS, T_SIZE, act_proj.shape[1])
    seq_blocks = jnp.einsum("sti,stj->sij", grad_seq, act_seq, preferred_element_type=jnp.float32)
    return jnp.sum(seq_blocks * seq_blocks, axis=0) / SEQS


def solution(mesh):
    return jax.shard_map(
        local,
        mesh=mesh,
        in_specs=(P("col", "grp"), P(None, "col"), P("grp", "col"), P("col", "grp")),
        out_specs=P("col", "grp"),
        check_vma=False,
    )
```

profile of v0, /device:TPU:6, one launch (start us, length us, event | category | flops | bytes accessed | tf_op | source)
XLA Modules:
  0.0 459.3 jit_solution(13343929270616797784)
XLA Ops:
  6.5 0.0 copy-start
  6.5 0.0 all-gather.2.cloned.1.call-start
  6.5 0.7 all-gather.2.cloned.1.call-update
  7.3 3.9 fusion.1
  11.2 354.2 %all-reduce.3 = bf16[1024,1024]{1,0:T(8,128)(2,1)} all-reduce(f32[1024,1024]{1,0:T(8,128)} %fusion.1), channel_id=1, replica_groups=mesh['grp'=8,'col'=64] {'col'}, use_global_device_ids=true, to_apply=%region_1.0 | all-reduce | flops 1048576 | bytes 6291456 | tf_op jit(solution)/shard_map/psum | solution.py:18
  365.3 0.0 all-gather.2.cloned.1.call-done
  365.3 0.0 copy-done
  365.3 7.3 %fusion = f32[1024,384]{1,0:T(8,128)} fusion(bf16[1024,3584]{1,0:T(8,128)(2,1)} %all-gather.2.cloned.1.call-done, bf16[3584,384]{1,0:T(8,128)(2,1)S(1)} %copy-done), kind=kOutput, calls=%fused_computation.2 | convolution fusion | flops 2818572288 | bytes 11665408 | tf_op jit(solution)/shard_map/dot_general | solution.py:11
  372.6 75.7 %all-reduce.2 = bf16[1024,384]{1,0:T(8,128)(2,1)S(1)} all-reduce(f32[1024,384]{1,0:T(8,128)} %fusion), channel_id=1, replica_groups=mesh['grp'=8,'col'=64] {'grp'}, use_global_device_ids=true, to_apply=%region_0.0 | all-reduce | flops 393216 | bytes 2359296 | tf_op jit(solution)/shard_map/psum | solution.py:16
  448.3 2.8 multiply_reduce_fusion
  451.2 1.3 broadcast_multiply_fusion
Async XLA Ops:
  6.5 358.8 %copy-start = (bf16[3584,384]{1,0:T(8,128)(2,1)S(1)}, bf16[3584,384]{1,0:T(8,128)(2,1)}, u32[]{:S(2)}) copy-start(bf16[3584,384]{1,0:T(8,128)(2,1)} %param.6) | copy-start | bytes 8257540
  6.5 358.8 %all-gather.2.cloned.1.call-start = ((), (), s32[]{:S(2)}) async-start(), calls=%async_computation | async-start | bytes 7454720 | tf_op jit(solution)/shard_map/all_gather | solution.py:12
Sparse Core Ops, SparseCore 0:
  10.7 113.1 all-gather.1
where the time goes:
time: 460 us; the launch traced here: 459 us
  blocking collectives  430 us (93%)
  matrix products  14.1 us (3%)
  between operations  13.4 us (3%)
    psum x1, blocking collectives, local(): act_proj = lax.psum(act_partial, 'col').astype(jnp.bfloat16)  354 us
    psum x1, blocking collectives, local(): grad_proj = lax.psum(grad_partial, 'grp').astype(jnp.bfloat16)  75.7 us
  transfers between devices with their start and end apart: 1, of which 0 were waited for; matrix products, arithmetic and copies ran while one was open for 1% of the time, Pallas kernels for 0%

commit v1 on v0

v1 whole, which is shorter than its diff:
```python
import jax
import jax.numpy as jnp
from jax import lax
from jax.sharding import Mesh, PartitionSpec as P

T_SIZE = 256
SEQS = 4
SWAP = [(0, 1), (1, 0)]
F32 = jnp.float32
BF16 = jnp.bfloat16


def dot(a, b):
    return jnp.dot(a, b, preferred_element_type=F32)


def spread(piece, axis, n):
    return lax.all_to_all(jnp.broadcast_to(piece[None], (n,) + piece.shape), axis, 0, 0)


def local(out_grads, in_acts, basis_out, basis_in):
    core = lax.axis_index("core")

    grads = lax.all_gather(out_grads, "zh", axis=0, tiled=True)
    grads = lax.all_gather(grads, "y", axis=0, tiled=True)
    basis_other = lax.ppermute(basis_out, "core", SWAP)

    acts = in_acts.reshape(8, 4, 2, 16, 128).transpose(0, 2, 1, 3, 4).reshape(1024, 128)
    acts = lax.all_gather(acts, "zh", axis=1, tiled=True)
    weights = lax.all_to_all(basis_in, "zh", 1, 0, tiled=True)
    here = lax.dynamic_slice_in_dim(weights, core * 128, 128, 1)
    there = lax.dynamic_slice_in_dim(weights, (1 - core) * 128, 128, 1)
    act = dot(acts, here) + lax.ppermute(dot(acts, there), "core", SWAP)
    act = lax.all_to_all(act.reshape(8, 128, 128), "y", 0, 0)
    act = jnp.sum(act, axis=0).astype(BF16)
    act = spread(act, "y", 8).reshape(1024, 128)
    act = lax.all_gather(act, "zh", axis=0)
    other = lax.ppermute(act, "core", SWAP)
    first = jnp.where(core == 0, act, other)
    second = jnp.where(core == 0, other, act)
    act = jnp.stack([first, second], axis=1)
    act = act.transpose(2, 0, 1, 3).reshape(SEQS, T_SIZE, 1024)

    both = reduce_both(dot(grads, basis_out), dot(grads, basis_other))
    own, sent = both[:, :384], both[:, 384:]
    got = lax.ppermute(sent, "core", SWAP)
    grad = jnp.stack([jnp.where(core == 0, own, got), jnp.where(core == 0, got, own)])
    grad = spread(grad, ("x", "zl"), 8).reshape(SEQS, T_SIZE, 384)

    blocks = jnp.einsum("sti,stj->sij", grad, act, preferred_element_type=F32)
    return jnp.sum(blocks * blocks, axis=0) / SEQS


def reduce_both(mine, others):
    partial = jnp.concatenate([mine, others], axis=1).astype(BF16)
    parts = lax.all_to_all(partial.reshape(8, 64, 768), ("x", "zl"), 0, 0)
    return jnp.sum(parts.astype(F32), axis=0).astype(BF16)


def solution(mesh):
    fine = Mesh(mesh.devices.reshape(4, 2, 8, 4, 2), ("x", "zl", "y", "zh", "core"))
    grp, col = ("x", "zl"), ("y", "zh", "core")
    return jax.shard_map(
        local,
        mesh=fine,
        in_specs=(P(col, grp), P(None, col), P(grp, col), P(col, grp)),
        out_specs=P(col, grp),
        check_vma=False,
    )
```

time: 460 us -> 206 us (0.45)
  the two profiles are of different devices: /device:TPU:6 before, /device:TPU:1 now
where the time goes in v1:
time: 206 us; the launch traced here: 205 us
  blocking collectives  96.9 us (47%)
  waiting for transfers between devices  46.7 us (23%)
  starting transfers between devices  22.5 us (11%)
  matrix products  14 us (7%)
  between operations  13.4 us (7%)
  local copies, waits for them, and re-layouts  9.71 us (5%)
    all_to_all x1, blocking collectives, reduce_both(): parts = lax.all_to_all(partial.reshape(8, 64, 768), ('x', 'zl'), 0, 0)  31.4 us
    all_to_all x1, blocking collectives, local(): act = lax.all_to_all(act.reshape(8, 128, 128), 'y', 0, 0)  27.6 us
    all_gather x1, blocking collectives, local(): grads = lax.all_gather(out_grads, 'zh', axis=0, tiled=True)  20.9 us
    all_to_all x1, blocking collectives, spread(): lax.all_to_all(jnp.broadcast_to(piece[None], (n,) + piece.shape), axis, 0...  17.1 us
    all_gather x1, waiting for transfers between devices, local(): grads = lax.all_gather(grads, 'y', axis=0, tiled=True)  16.9 us
    all_gather x1, waiting for transfers between devices, local(): acts = lax.all_gather(acts, 'zh', axis=1, tiled=True)  16.7 us
    dot_general x4, matrix products, dot(): return jnp.dot(a, b, preferred_element_type=F32)  11.2 us
    all_to_all x1, waiting for transfers between devices, spread(): lax.all_to_all(jnp.broadcast_to(piece[None], (n,) + piece.shape), axis, 0...  7.22 us
  transfers between devices with their start and end apart: 9, of which 5 were waited for; matrix products, arithmetic and copies ran while one was open for 10% of the time, Pallas kernels for 0%

profile of v1, /device:TPU:1, one launch (start us, length us, event | category | flops | bytes accessed | tf_op | source)
XLA Modules:
  0.0 205.0 jit_solution(10211206331671415686)
XLA Ops:
  6.5 1.7 copy.15
  8.3 20.9 %all_gather.12 = bf16[64,3584]{1,0:T(8,128)(2,1)} all-gather(bf16[16,3584]{1,0:T(8,128)(2,1)} %param.4), channel_id=1, replica_groups=mesh['x'=4,'zl'=2,'y'=8,'zh'=4,'core'=2] {'zh'}, dimensions={0}, use_global_device_ids=true | all-gather | bytes 573440 | tf_op jit(solution)/shard_map/all_gather | solution.py:24
  29.2 1.8 copy.13
  31.0 3.4 %all-to-all-start.2 = ((bf16[128,4,256]{0,2,1:T(8,128)(2,1)}), bf16[128,4,256]{0,2,1:T(8,128)(2,1)S(1)}, u32[]{:S(2)}, u32[]{:S(2)}) async-start(bf16[128,4,256]{0,2,1:T(8,128)(2,1)} %bitcast.5), calls=%async_computation.2 | async-start | bytes 524288 | tf_op jit(solution)/shard_map/all_to_all | solution.py:30
  34.5 6.0 %collective-permute-start = (bf16[3584,384]{1,0:T(8,128)(2,1)}, bf16[3584,384]{1,0:T(8,128)(2,1)}, u32[]{:S(2)}, u32[]{:S(2)}) collective-permute-start(bf16[3584,384]{1,0:T(8,128)(2,1)} %param.6), channel_id=1, source_target_pairs={{0,1},{1,0},{2,3},{3,2},{4,5},{5,4},{6,7},{7,6},{8,9},{9,8},{10,11... | collective-permute-start | bytes 8257544 | tf_op jit(solution)/shard_map/ppermute | solution.py:26
  40.4 4.2 %all-to-all-done.2 = bf16[128,4,256]{0,2,1:T(8,128)(2,1)S(1)} async-done(((bf16[128,4,256]{0,2,1:T(8,128)(2,1)}), bf16[128,4,256]{0,2,1:T(8,128)(2,1)S(1)}, u32[]{:S(2)}, u32[]{:S(2)}) %all-to-all-start.2) | async-done | bytes 262176 | tf_op jit(solution)/shard_map/all_to_all | solution.py:30
  44.6 0.1 copy.14
  44.8 16.7 %all-gather.6.cloned.1.call-done = bf16[1024,512]{1,0:T(8,128)(2,1)} async-done(((bf16[1024,128]{1,0:T(8,128)(2,1)}), bf16[1024,512]{1,0:T(8,128)(2,1)}) %all-gather.6.cloned.1.call-update) | async-done | bytes 1048592 | tf_op jit(solution)/shard_map/all_gather | solution.py:29
  61.5 1.8 convolution_bitcast_fusion
  63.3 2.4 %collective-permute-start.2 = (f32[1024,128]{0,1:T(8,128)S(1)}, f32[1024,128]{0,1:T(8,128)S(1)}, u32[]{:S(2)}, u32[]{:S(2)}) collective-permute-start(f32[1024,128]{0,1:T(8,128)S(1)} %convolution_bitcast_fusion), channel_id=1, source_target_pairs={{0,1},{1,0},{2,3},{3,2},{4,5},{5,4},{6,7},{7,6},{8,9},{9,8},{10,11... | collective-permute-start | bytes 1572872 | tf_op jit(solution)/shard_map/ppermute | solution.py:33
  65.7 1.5 collective-permute-done.2
  67.2 0.5 fusion.1
  67.8 27.6 %all_to_all.39 = f32[8,128,128]{1,2,0:T(8,128)S(1)} all-to-all(f32[8,128,128]{1,2,0:T(8,128)S(1)} %bitcast.42), channel_id=1, replica_groups=mesh['x'=4,'zl'=2,'y'=8,'zh'=4,'core'=2] {'y'}, dimensions={0} | all-to-all | bytes 1048576 | tf_op jit(solution)/shard_map/all_to_all | solution.py:34
  95.4 0.1 copy.18
  95.5 17.1 %all_to_all.40 = bf16[8,128,128]{2,1,0:T(8,128)(2,1)} all-to-all(bf16[8,128,128]{2,1,0:T(8,128)(2,1)S(1)} %broadcast_in_dim.5), channel_id=1, replica_groups=mesh['x'=4,'zl'=2,'y'=8,'zh'=4,'core'=2] {'y'}, dimensions={0} | all-to-all | bytes 524288 | tf_op jit(solution)/shard_map/all_to_all | solution.py:18
  112.6 16.9 %all-gather.4.cloned.1.call-done = bf16[512,3584]{1,0:T(8,128)(2,1)} async-done(((bf16[64,3584]{1,0:T(8,128)(2,1)}), bf16[512,3584]{1,0:T(8,128)(2,1)}) %all-gather.4.cloned.1.call-update) | async-done | bytes 3670032 | tf_op jit(solution)/shard_map/all_gather | solution.py:25
  129.6 5.1 %convolution_convert_fusion.1 = bf16[512,384]{1,0:T(8,128)(2,1)S(1)} fusion(bf16[512,3584]{1,0:T(8,128)(2,1)} %all-gather.4.cloned.1.call-done, bf16[3584,384]{1,0:T(8,128)(2,1)} %param.6), kind=kOutput, calls=%fused_computation.3 | convolution fusion | flops 1409482752 | bytes 6815744 | tf_op jit(solution)/shard_map/dot_general | solution.py:14
  134.7 3.8 %convolution_convert_fusion = bf16[512,384]{1,0:T(8,128)(2,1)S(1)} fusion(bf16[512,3584]{1,0:T(8,128)(2,1)S(1)} %copy-done.2, bf16[3584,384]{1,0:T(8,128)(2,1)} %collective-permute-done), kind=kOutput, calls=%fused_computation.2 | convolution fusion | flops 1409482752 | bytes 6815744 | tf_op jit(solution)/shard_map/dot_general | solution.py:14
  138.5 0.1 pad_maximum_fusion
  138.6 31.4 %all_to_all.41 = bf16[8,64,768]{2,1,0:T(8,128)(2,1)S(1)} all-to-all(bf16[8,64,768]{2,1,0:T(8,128)(2,1)S(1)} %pad_maximum_fusion), channel_id=1, replica_groups=mesh['x'=4,'zl'=2,'y'=8,'zh'=4,'core'=2] {'x','zl'}, dimensions={0} | all-to-all | bytes 1572864 | tf_op jit(solution)/shard_map/all_to_all | solution.py:56
  170.0 0.1 reduce_sum.30
  170.1 5.0 %collective-permute-start.1 = (bf16[64,384]{1,0:T(8,128)(2,1)S(1)}, bf16[64,384]{1,0:T(8,128)(2,1)S(1)}, u32[]{:S(2)}, u32[]{:S(2)}) collective-permute-start(bf16[64,384]{1,0:T(8,128)(2,1)S(1)} %slice.9), channel_id=1, source_target_pairs={{0,1},{1,0},{2,3},{3,2},{4,5},{5,4},{6,7},{7,6},{8,9},{9,8},{10,11... | collective-permute-start | bytes 147464 | tf_op jit(solution)/shard_map/ppermute | solution.py:46
  175.2 2.1 %collective-permute-start.3 = (bf16[4,1024,128]{2,1,0:T(8,128)(2,1)}, bf16[4,1024,128]{2,1,0:T(8,128)(2,1)S(1)}, u32[]{:S(2)}, u32[]{:S(2)}) collective-permute-start(bf16[4,1024,128]{2,1,0:T(8,128)(2,1)} %all-gather.8.cloned.1.call-done), channel_id=1, source_target_pairs={{0,1},{1,0},{2,3},{3,2},{4,5},{5,4},{6,7},{7,6},{8,9},{9,8},{10,11... | collective-permute-start | bytes 3145736 | tf_op jit(solution)/shard_map/ppermute | solution.py:38
  177.3 1.0 broadcast_in_dim.4
  178.3 3.5 %all-to-all-start.1 = ((bf16[8,2,64,384]{3,2,1,0:T(8,128)(2,1)}), bf16[8,2,64,384]{3,2,1,0:T(8,128)(2,1)S(1)}, u32[]{:S(2)}, u32[]{:S(2)}) async-start(bf16[8,2,64,384]{3,2,1,0:T(8,128)(2,1)} %broadcast_in_dim.4), calls=%async_computation.1 | async-start | bytes 1572864 | tf_op jit(solution)/shard_map/all_to_all | solution.py:18
  181.9 0.1 select_bitcast_fusion.1
  182.0 0.2 maximum_bitcast_fusion
  182.2 2.2 %copy.19 = bf16[1024,4,2,128]{3,2,1,0:T(2,128)(2,1)S(1)} copy(bf16[1024,4,2,128]{3,0,1,2:T(8,128)(2,1)S(1)} %maximum_bitcast_fusion) | data formatting | bytes 4194304 | tf_op jit(solution)/shard_map/transpose | solution.py:42
  184.4 2.7 %reshape.31 = bf16[4,256,1024]{2,1,0:T(8,128)(2,1)} reshape(bf16[1024,4,2,128]{3,2,1,0:T(2,128)(2,1)S(1)} %copy.19) | data formatting | bytes 4194304 | tf_op jit(solution)/shard_map/reshape | solution.py:42
  187.1 7.2 %all-to-all-done.1 = bf16[8,2,64,384]{3,2,1,0:T(8,128)(2,1)S(1)} async-done(((bf16[8,2,64,384]{3,2,1,0:T(8,128)(2,1)}), bf16[8,2,64,384]{3,2,1,0:T(8,128)(2,1)S(1)}, u32[]{:S(2)}, u32[]{:S(2)}) %all-to-all-start.1) | async-done | bytes 786464 | tf_op jit(solution)/shard_map/all_to_all | solution.py:18
  194.3 2.8 %multiply_reduce_fusion = f32[384,1024]{1,0:T(8,128)S(1)} fusion(bf16[4,256,384]{2,1,0:T(8,128)(2,1)S(1)} %bitcast.48, bf16[4,256,1024]{2,1,0:T(8,128)(2,1)} %reshape.31), kind=kOutput, calls=%fused_computation | convolution fusion | flops 808058880 | bytes 4456448 | tf_op jit(solution)/shard_map/sti,stj->sij/dot_general | solution.py:50
  197.2 1.3 broadcast_multiply_fusion
  (22 shorter events, 0.3 us)
Async XLA Ops:
  6.5 55.0 %all-gather.6.cloned.1.call-start = ((), (), s32[]{:S(2)}) async-start(), calls=%async_computation.6 | async-start | bytes 1310720 | tf_op jit(solution)/shard_map/all_gather | solution.py:29
  8.2 121.3 %all-gather.4.cloned.1.call-start = ((), (), s32[]{:S(2)}) async-start(), calls=%async_computation.5 | async-start | bytes 4128768 | tf_op jit(solution)/shard_map/all_gather | solution.py:25
  31.0 13.6 %all-to-all-start.2 = ((bf16[128,4,256]{0,2,1:T(8,128)(2,1)}), bf16[128,4,256]{0,2,1:T(8,128)(2,1)S(1)}, u32[]{:S(2)}, u32[]{:S(2)}) async-start(bf16[128,4,256]{0,2,1:T(8,128)(2,1)} %bitcast.5), calls=%async_computation.2 | async-start | bytes 524288 | tf_op jit(solution)/shard_map/all_to_all | solution.py:30
  34.5 140.7 %all-gather.8.cloned.1.call-start = ((), (), s32[]{:S(2)}) async-start(), calls=%async_computation.7 | async-start | bytes 1310720 | tf_op jit(solution)/shard_map/all_gather | solution.py:37
  34.5 100.2 %collective-permute-start = (bf16[3584,384]{1,0:T(8,128)(2,1)}, bf16[3584,384]{1,0:T(8,128)(2,1)}, u32[]{:S(2)}, u32[]{:S(2)}) collective-permute-start(bf16[3584,384]{1,0:T(8,128)(2,1)} %param.6), channel_id=1, source_target_pairs={{0,1},{1,0},{2,3},{3,2},{4,5},{5,4},{6,7},{7,6},{8,9},{9,8},{10,11... | collective-permute-start | bytes 8257544 | tf_op jit(solution)/shard_map/ppermute | solution.py:26
  61.5 5.7 %copy-start = (bf16[1024,512]{1,0:T(8,128)(2,1)S(1)}, bf16[1024,512]{1,0:T(8,128)(2,1)}, u32[]{:S(2)}) copy-start(bf16[1024,512]{1,0:T(8,128)(2,1)} %all-gather.6.cloned.1.call-done) | copy-start | bytes 3145732
  63.3 3.9 %collective-permute-start.2 = (f32[1024,128]{0,1:T(8,128)S(1)}, f32[1024,128]{0,1:T(8,128)S(1)}, u32[]{:S(2)}, u32[]{:S(2)}) collective-permute-start(f32[1024,128]{0,1:T(8,128)S(1)} %convolution_bitcast_fusion), channel_id=1, source_target_pairs={{0,1},{1,0},{2,3},{3,2},{4,5},{5,4},{6,7},{7,6},{8,9},{9,8},{10,11... | collective-permute-start | bytes 1572872 | tf_op jit(solution)/shard_map/ppermute | solution.py:33
  129.6 5.1 %copy-start.2 = (bf16[512,3584]{1,0:T(8,128)(2,1)S(1)}, bf16[512,3584]{1,0:T(8,128)(2,1)}, u32[]{:S(2)}) copy-start(bf16[512,3584]{1,0:T(8,128)(2,1)} %all-gather.4.cloned.1.call-done) | copy-start | bytes 11010052
  170.1 7.2 %collective-permute-start.1 = (bf16[64,384]{1,0:T(8,128)(2,1)S(1)}, bf16[64,384]{1,0:T(8,128)(2,1)S(1)}, u32[]{:S(2)}, u32[]{:S(2)}) collective-permute-start(bf16[64,384]{1,0:T(8,128)(2,1)S(1)} %slice.9), channel_id=1, source_target_pairs={{0,1},{1,0},{2,3},{3,2},{4,5},{5,4},{6,7},{7,6},{8,9},{9,8},{10,11... | collective-permute-start | bytes 147464 | tf_op jit(solution)/shard_map/ppermute | solution.py:46
  175.2 6.7 %copy-start.1 = (bf16[4,1024,128]{2,1,0:T(8,128)(2,1)S(1)}, bf16[4,1024,128]{2,1,0:T(8,128)(2,1)}, u32[]{:S(2)}) copy-start(bf16[4,1024,128]{2,1,0:T(8,128)(2,1)} %all-gather.8.cloned.1.call-done) | copy-start | bytes 3145732
  175.2 6.7 %collective-permute-start.3 = (bf16[4,1024,128]{2,1,0:T(8,128)(2,1)}, bf16[4,1024,128]{2,1,0:T(8,128)(2,1)S(1)}, u32[]{:S(2)}, u32[]{:S(2)}) collective-permute-start(bf16[4,1024,128]{2,1,0:T(8,128)(2,1)} %all-gather.8.cloned.1.call-done), channel_id=1, source_target_pairs={{0,1},{1,0},{2,3},{3,2},{4,5},{5,4},{6,7},{7,6},{8,9},{9,8},{10,11... | collective-permute-start | bytes 3145736 | tf_op jit(solution)/shard_map/ppermute | solution.py:38
  178.3 16.0 %all-to-all-start.1 = ((bf16[8,2,64,384]{3,2,1,0:T(8,128)(2,1)}), bf16[8,2,64,384]{3,2,1,0:T(8,128)(2,1)S(1)}, u32[]{:S(2)}, u32[]{:S(2)}) async-start(bf16[8,2,64,384]{3,2,1,0:T(8,128)(2,1)} %broadcast_in_dim.4), calls=%async_computation.1 | async-start | bytes 1572864 | tf_op jit(solution)/shard_map/all_to_all | solution.py:18
Sparse Core Ops, SparseCore 0:
  9.4 52.0 all-gather.5
  63.6 65.9 all-gather.3
  131.7 40.8 all-gather.7

commit v2 on v0

v2 whole, which is shorter than its diff:
```python
import jax
import jax.numpy as jnp
from jax import lax
from jax.experimental import pallas as pl
from jax.experimental.pallas import tpu as pltpu
from jax.sharding import Mesh, PartitionSpec as P

SEQS = 4
SWAP = [(0, 1), (1, 0)]
GRP = ("x", "zl")
F32 = jnp.float32
BF16 = jnp.bfloat16
PARAMS = pltpu.CompilerParams(vmem_limit_bytes=40 * 1024 * 1024)


def dot(a, b):
    return jnp.dot(a, b, preferred_element_type=F32)


def exchange(pieces, axis):
    return lax.all_to_all(pieces, axis, 0, 0)


def spread(piece, axis, n):
    return exchange(jnp.broadcast_to(piece[None], (n,) + piece.shape), axis)


def grad_kernel(grads_ref, mine_ref, other_ref, out_ref, acc_ref):
    step = pl.program_id(0)
    mine = dot(grads_ref[...], mine_ref[...])
    other = dot(grads_ref[...], other_ref[...])

    @pl.when(step == 0)
    def _():
        acc_ref[:, :384] = mine
        acc_ref[:, 384:] = other

    @pl.when(step > 0)
    def _():
        acc_ref[:, :384] += mine
        acc_ref[:, 384:] += other

    @pl.when(step == pl.num_programs(0) - 1)
    def _():
        out_ref[...] = acc_ref[...].astype(BF16)


def project_grads(grads, mine, other):
    depth = 512
    return pl.pallas_call(
        grad_kernel,
        grid=(grads.shape[1] // depth,),
        in_specs=[
            pl.BlockSpec((512, depth), lambda k: (0, k)),
            pl.BlockSpec((depth, 384), lambda k: (k, 0)),
            pl.BlockSpec((depth, 384), lambda k: (k, 0)),
        ],
        out_specs=pl.BlockSpec((512, 768), lambda k: (0, 0)),
        out_shape=jax.ShapeDtypeStruct((512, 768), BF16),
        scratch_shapes=[pltpu.VMEM((512, 768), F32)],
        compiler_params=PARAMS,
        name="project_grads",
    )(grads, mine, other)


def act_kernel(core_ref, gathered_ref, here_ref, there_ref):
    core = core_ref[0]
    here = there = None
    for z in range(4):
        acts = gathered_ref[z, :1024, :]
        low = dot(acts, gathered_ref[z, 1024:1152, :])
        high = dot(acts, gathered_ref[z, 1152:1280, :])
        here = low if z == 0 else here + low
        there = high if z == 0 else there + high
    first = core == 0
    here_ref[...] = jnp.where(first, here, there)
    there_ref[...] = jnp.where(first, there, here)


def project_acts(core, gathered):
    half = jax.ShapeDtypeStruct((1024, 128), F32)
    return pl.pallas_call(
        act_kernel,
        in_specs=[
            pl.BlockSpec(memory_space=pltpu.SMEM),
            pl.BlockSpec(memory_space=pltpu.VMEM),
        ],
        out_specs=[pl.BlockSpec(memory_space=pltpu.VMEM)] * 2,
        out_shape=[half, half],
        compiler_params=PARAMS,
        name="project_acts",
    )(core, gathered)


def fit_kernel(core_ref, grad_ref, mine_ref, other_ref, out_ref):
    first = core_ref[0] == 0
    for half in range(2):
        keep = first if half == 0 else jnp.logical_not(first)
        total = None
        for s in range(SEQS):
            mine = mine_ref[2 * s : 2 * s + 2, 0].reshape(256, 128)
            other = other_ref[2 * s : 2 * s + 2, 0].reshape(256, 128)
            act = jnp.where(keep, mine, other)
            grad = grad_ref[256 * s : 256 * s + 256, :]
            block = lax.dot_general(grad, act, (((0,), (0,)), ((), ())), preferred_element_type=F32)
            total = block * block if s == 0 else total + block * block
        out_ref[:, 128 * half : 128 * half + 128] = total * (1.0 / SEQS)


def fit(core, grad, mine, other):
    acts = pl.BlockSpec((8, 1, 128, 128), lambda z: (0, z, 0, 0))
    return pl.pallas_call(
        fit_kernel,
        grid=(4,),
        in_specs=[
            pl.BlockSpec(memory_space=pltpu.SMEM),
            pl.BlockSpec((1024, 384), lambda z: (0, 0)),
            acts,
            acts,
        ],
        out_specs=pl.BlockSpec((384, 256), lambda z: (0, z)),
        out_shape=jax.ShapeDtypeStruct((384, 1024), F32),
        compiler_params=PARAMS,
        name="fit_blocks",
    )(core, grad, mine, other)


def local(out_grads, in_acts, basis_out, basis_in):
    core = lax.axis_index("core")
    core_arr = core.astype(jnp.int32).reshape(1)

    grads = lax.all_gather(out_grads, "zh", axis=0, tiled=True)
    grads, in_acts, basis_out, basis_in = lax.optimization_barrier((grads, in_acts, basis_out, basis_in))
    grads = lax.all_gather(grads, "y", axis=0, tiled=True)
    basis_other = lax.ppermute(basis_out, "core", SWAP)

    halves = basis_in.reshape(128, 8, 128).transpose(1, 0, 2).reshape(4, 256, 128)
    pieces = jnp.concatenate([jnp.broadcast_to(in_acts[None], (4, 1024, 128)), halves], axis=1)
    here, there = project_acts(core_arr, exchange(pieces, "zh"))
    act = here + lax.ppermute(there, "core", SWAP)
    act = jnp.sum(exchange(act.reshape(8, 128, 128), "y"), axis=0).astype(BF16)
    act = act.reshape(4, 2, 16, 128).transpose(1, 0, 2, 3).reshape(128, 128)
    act = spread(act, ("y", "zh"), 32).reshape(8, 4, 128, 128)
    act_other = lax.ppermute(act, "core", SWAP)

    partial = project_grads(grads, basis_out, basis_other)
    parts = exchange(partial.reshape(8, 64, 768), GRP)
    both = jnp.sum(parts.astype(F32), axis=0).astype(BF16)
    own = both[:, :384]
    got = lax.ppermute(both[:, 384:], "core", SWAP)
    grad = jnp.concatenate([jnp.where(core == 0, own, got), jnp.where(core == 0, got, own)])
    grad = spread(grad, GRP, 8).reshape(1024, 384)

    return fit(core_arr, grad, act, act_other)


def solution(mesh):
    fine = Mesh(mesh.devices.reshape(4, 2, 8, 4, 2), ("x", "zl", "y", "zh", "core"))
    col = ("y", "zh", "core")
    return jax.shard_map(
        local,
        mesh=fine,
        in_specs=(P(col, GRP), P(None, col), P(GRP, col), P(col, GRP)),
        out_specs=P(col, GRP),
        check_vma=False,
    )
```

time: 460 us -> 182 us (0.40)
  the two profiles are of different devices: /device:TPU:6 before, /device:TPU:8 now
where the time goes in v2:
time: 182 us; the launch traced here: 181 us
  waiting for transfers between devices  86.8 us (48%)
  starting transfers between devices  35.7 us (20%)
  blocking collectives  22.7 us (12%)
  between operations  13.5 us (7%)
  Pallas kernels  12.7 us (7%)
  local copies, waits for them, and re-layouts  7.12 us (4%)
  other arithmetic  2.19 us (1%)
    all_to_all x5, waiting for transfers between devices, exchange(): return lax.all_to_all(pieces, axis, 0, 0)  63.1 us
    all_to_all x5, starting transfers between devices, exchange(): return lax.all_to_all(pieces, axis, 0, 0)  28 us
    all_gather x1, blocking collectives, local(): grads = lax.all_gather(out_grads, 'zh', axis=0, tiled=True)  22.7 us
    all_gather x1, waiting for transfers between devices, local(): grads = lax.all_gather(grads, 'y', axis=0, tiled=True)  18 us
    pallas_call x1, Pallas kernels, project_grads(): pl.pallas_call(grad_kernel, grid=(grads.shape[1] // depth,), in_specs=[pl...  8.54 us
    unnamed x6, local copies, waits for them, and re-layouts  3.82 us
  transfers between devices with their start and end apart: 10, of which 8 were waited for; matrix products, arithmetic and copies ran while one was open for 2% of the time, Pallas kernels for 5%

profile of v2, /device:TPU:8, one launch (start us, length us, event | category | flops | bytes accessed | tf_op | source)
XLA Modules:
  0.0 180.7 jit_solution(5370315319412910535)
XLA Ops:
  6.5 22.7 %all_gather.6 = bf16[64,3584]{1,0:T(8,128)(2,1)} all-gather(bf16[16,3584]{1,0:T(8,128)(2,1)} %param.4), channel_id=1, replica_groups=mesh['x'=4,'zl'=2,'y'=8,'zh'=4,'core'=2] {'zh'}, dimensions={0}, use_global_device_ids=true | all-gather | bytes 573440 | tf_op jit(solution)/shard_map/all_gather | solution.py:132
  29.3 0.0 all-gather.2.cloned.1.call-update
  29.4 1.1 broadcast_in_dim.9
  30.4 1.1 pad_maximum_fusion
  31.6 4.3 %all-to-all-start.2 = ((bf16[4,1280,128]{2,1,0:T(8,128)(2,1)}), bf16[4,1280,128]{2,1,0:T(8,128)(2,1)S(1)}, u32[]{:S(2)}, u32[]{:S(2)}) async-start(bf16[4,1280,128]{2,1,0:T(8,128)(2,1)} %pad_maximum_fusion), calls=%async_computation.2 | async-start | bytes 2621440 | tf_op jit(solution)/shard_map/all_to_all | solution.py:21
  35.9 1.9 %collective-permute-start = (bf16[3584,384]{1,0:T(8,128)(2,1)}, bf16[3584,384]{1,0:T(8,128)(2,1)}, u32[]{:S(2)}, u32[]{:S(2)}) collective-permute-start(bf16[3584,384]{1,0:T(8,128)(2,1)} %mine_ref), channel_id=1, source_target_pairs={{0,1},{1,0},{2,3},{3,2},{4,5},{5,4},{6,7},{7,6},{8,9},{9,8},{10,11... | collective-permute-start | bytes 8257544 | tf_op jit(solution)/shard_map/ppermute | solution.py:135
  37.8 20.2 %all-to-all-done.2.gathered_ref = bf16[4,1280,128]{2,1,0:T(8,128)(2,1)S(1)} async-done(((bf16[4,1280,128]{2,1,0:T(8,128)(2,1)}), bf16[4,1280,128]{2,1,0:T(8,128)(2,1)S(1)}, u32[]{:S(2)}, u32[]{:S(2)}) %all-to-all-start.2) | async-done | bytes 1310752 | tf_op jit(solution)/shard_map/all_to_all | solution.py:21
  58.0 0.7 project_acts.1
  58.7 1.9 %collective-permute-start.2 = (f32[1024,128]{1,0:T(8,128)S(1)}, f32[1024,128]{1,0:T(8,128)S(1)}, u32[]{:S(2)}, u32[]{:S(2)}) collective-permute-start(f32[1024,128]{1,0:T(8,128)S(1)} %get-tuple-element.16), channel_id=1, source_target_pairs={{0,1},{1,0},{2,3},{3,2},{4,5},{5,4},{6,7},{7,6},{8,9},{9,8},{10,11... | collective-permute-start | bytes 1572872 | tf_op jit(solution)/shard_map/ppermute | solution.py:140
  60.6 1.9 %collective-permute-done.2 = f32[1024,128]{1,0:T(8,128)S(1)} collective-permute-done((f32[1024,128]{1,0:T(8,128)S(1)}, f32[1024,128]{1,0:T(8,128)S(1)}, u32[]{:S(2)}, u32[]{:S(2)}) %collective-permute-start.2) | collective-permute-done | bytes 524320 | tf_op jit(solution)/shard_map/ppermute | solution.py:140
  62.5 0.9 add.3
  63.4 7.5 %all-to-all-start.3 = ((f32[8,128,128]{2,1,0:T(8,128)}), f32[8,128,128]{2,1,0:T(8,128)S(1)}, u32[]{:S(2)}, u32[]{:S(2)}) async-start(f32[8,128,128]{2,1,0:T(8,128)} %bitcast.5), calls=%async_computation.3 | async-start | bytes 1048576 | tf_op jit(solution)/shard_map/all_to_all | solution.py:21
  70.9 0.0 collective-permute-done.other_ref
  70.9 18.0 %all-gather.2.cloned.1.call-done.grads_ref = bf16[512,3584]{1,0:T(8,128)(2,1)} async-done(((bf16[64,3584]{1,0:T(8,128)(2,1)}), bf16[512,3584]{1,0:T(8,128)(2,1)}) %all-gather.2.cloned.1.call-update) | async-done | bytes 3670032 | tf_op jit(solution)/shard_map/all_gather | solution.py:134
  89.0 2.0 %copy-done.1 = bf16[512,3584]{1,0:T(8,128)(2,1)S(1)} copy-done((bf16[512,3584]{1,0:T(8,128)(2,1)S(1)}, bf16[512,3584]{1,0:T(8,128)(2,1)}, u32[]{:S(2)}) %copy-start.1) | copy-done | bytes 3670040
  91.0 1.8 copy-done.2
  92.8 8.5 %project_grads.1 = bf16[512,768]{1,0:T(8,128)(2,1)} custom-call(bf16[512,3584]{1,0:T(8,128)(2,1)S(1)} %copy-done.1, bf16[3584,384]{1,0:T(8,128)(2,1)S(1)} %copy-done.2, bf16[3584,384]{1,0:T(8,128)(2,1)} %collective-permute-done.other_ref), custom_call_target="tpu_custom_call" | custom-call | tf_op jit(solution)/shard_map/project_grads/pallas_call | solution.py:50
  101.3 0.0 all-to-all-done.3
  101.3 4.2 %all-to-all-start = ((bf16[8,64,768]{2,1,0:T(8,128)(2,1)}), bf16[8,64,768]{2,1,0:T(8,128)(2,1)S(1)}, u32[]{:S(2)}, u32[]{:S(2)}) async-start(bf16[8,64,768]{2,1,0:T(8,128)(2,1)} %bitcast.1), calls=%async_computation | async-start | bytes 1572864 | tf_op jit(solution)/shard_map/all_to_all | solution.py:21
  105.6 12.3 %all-to-all-done = bf16[8,64,768]{2,1,0:T(8,128)(2,1)S(1)} async-done(((bf16[8,64,768]{2,1,0:T(8,128)(2,1)}), bf16[8,64,768]{2,1,0:T(8,128)(2,1)S(1)}, u32[]{:S(2)}, u32[]{:S(2)}) %all-to-all-start) | async-done | bytes 786464 | tf_op jit(solution)/shard_map/all_to_all | solution.py:21
  118.0 1.2 broadcast_in_dim.22
  119.2 8.3 %all-to-all-start.4 = ((bf16[32,128,128]{2,1,0:T(8,128)(2,1)}), bf16[32,128,128]{2,1,0:T(8,128)(2,1)S(1)}, u32[]{:S(2)}, u32[]{:S(2)}) async-start(bf16[32,128,128]{2,1,0:T(8,128)(2,1)} %broadcast_in_dim.22), calls=%async_computation.4 | async-start | bytes 2097152 | tf_op jit(solution)/shard_map/all_to_all | solution.py:21
  127.5 0.1 reduce_sum.21
  127.6 1.9 %collective-permute-start.1 = (bf16[64,384]{1,0:T(8,128)(2,1)S(1)}, bf16[64,384]{1,0:T(8,128)(2,1)S(1)}, u32[]{:S(2)}, u32[]{:S(2)}) collective-permute-start(bf16[64,384]{1,0:T(8,128)(2,1)S(1)} %slice.9), channel_id=1, source_target_pairs={{0,1},{1,0},{2,3},{3,2},{4,5},{5,4},{6,7},{7,6},{8,9},{9,8},{10,11... | collective-permute-start | bytes 147464 | tf_op jit(solution)/shard_map/ppermute | solution.py:150
  129.5 1.2 collective-permute-done.1
  130.8 24.9 %all-to-all-done.4 = bf16[32,128,128]{2,1,0:T(8,128)(2,1)S(1)} async-done(((bf16[32,128,128]{2,1,0:T(8,128)(2,1)}), bf16[32,128,128]{2,1,0:T(8,128)(2,1)S(1)}, u32[]{:S(2)}, u32[]{:S(2)}) %all-to-all-start.4) | async-done | bytes 1048608 | tf_op jit(solution)/shard_map/all_to_all | solution.py:21
  155.7 0.9 broadcast_in_dim.8
  156.6 3.7 %all-to-all-start.1 = ((bf16[8,128,384]{2,1,0:T(8,128)(2,1)}), bf16[8,128,384]{2,1,0:T(8,128)(2,1)S(1)}, u32[]{:S(2)}, u32[]{:S(2)}) async-start(bf16[8,128,384]{2,1,0:T(8,128)(2,1)} %broadcast_in_dim.8), calls=%async_computation.1 | async-start | bytes 1572864 | tf_op jit(solution)/shard_map/all_to_all | solution.py:21
  160.3 1.9 %collective-permute-start.3 = (bf16[8,4,128,128]{3,2,1,0:T(8,128)(2,1)S(1)}, bf16[8,4,128,128]{3,2,1,0:T(8,128)(2,1)S(1)}, u32[]{:S(2)}, u32[]{:S(2)}) collective-permute-start(bf16[8,4,128,128]{3,2,1,0:T(8,128)(2,1)S(1)} %bitcast.17), channel_id=1, source_target_pairs={{0,1},{1,0},{2,3},{3,2},{4,5},{5,4},{6,7},{7,6},{8,9},{9,8},{10,11... | collective-permute-start | bytes 3145736 | tf_op jit(solution)/shard_map/ppermute | solution.py:144
  162.2 2.6 %collective-permute-done.3.other_ref = bf16[8,4,128,128]{3,2,1,0:T(8,128)(2,1)S(1)} collective-permute-done((bf16[8,4,128,128]{3,2,1,0:T(8,128)(2,1)S(1)}, bf16[8,4,128,128]{3,2,1,0:T(8,128)(2,1)S(1)}, u32[]{:S(2)}, u32[]{:S(2)}) %collective-permute-start.3) | collective-permute-done | bytes 1048608 | tf_op jit(solution)/shard_map/ppermute | solution.py:144
  164.8 5.6 %all-to-all-done.1 = bf16[8,128,384]{2,1,0:T(8,128)(2,1)S(1)} async-done(((bf16[8,128,384]{2,1,0:T(8,128)(2,1)}), bf16[8,128,384]{2,1,0:T(8,128)(2,1)S(1)}, u32[]{:S(2)}, u32[]{:S(2)}) %all-to-all-start.1) | async-done | bytes 786464 | tf_op jit(solution)/shard_map/all_to_all | solution.py:21
  170.4 3.5 %fit_blocks.1 = f32[384,1024]{1,0:T(8,128)} custom-call(s32[1]{0:T(128)} %bitcast.core_ref, bf16[1024,384]{1,0:T(8,128)(2,1)S(1)} %bitcast.19, bf16[8,4,128,128]{3,2,1,0:T(8,128)(2,1)S(1)} %bitcast.18, bf16[8,4,128,128]{3,2,1,0:T(8,128)(2,1)S(1)} %collective-permute-done.3.other_ref), custom_call_target="tpu_custom_call" | custom-call | tf_op jit(solution)/shard_map/fit_blocks/pallas_call | solution.py:112
  (11 shorter events, 0.1 us)
Async XLA Ops:
  6.5 22.8 %copy-start = (bf16[128,1024]{1,0:T(8,128)(2,1)S(1)}, bf16[128,1024]{1,0:T(8,128)(2,1)}, u32[]{:S(2)}) copy-start(bf16[128,1024]{1,0:T(8,128)(2,1)} %param.7) | copy-start | bytes 786436
  6.5 82.4 %all-gather.2.cloned.1.call-start = ((), (), s32[]{:S(2)}) async-start(), calls=%async_computation.5 | async-start | bytes 4128768 | tf_op jit(solution)/shard_map/all_gather | solution.py:134
  31.6 26.4 %all-to-all-start.2 = ((bf16[4,1280,128]{2,1,0:T(8,128)(2,1)}), bf16[4,1280,128]{2,1,0:T(8,128)(2,1)S(1)}, u32[]{:S(2)}, u32[]{:S(2)}) async-start(bf16[4,1280,128]{2,1,0:T(8,128)(2,1)} %pad_maximum_fusion), calls=%async_computation.2 | async-start | bytes 2621440 | tf_op jit(solution)/shard_map/all_to_all | solution.py:21
  35.9 35.1 %collective-permute-start = (bf16[3584,384]{1,0:T(8,128)(2,1)}, bf16[3584,384]{1,0:T(8,128)(2,1)}, u32[]{:S(2)}, u32[]{:S(2)}) collective-permute-start(bf16[3584,384]{1,0:T(8,128)(2,1)} %mine_ref), channel_id=1, source_target_pairs={{0,1},{1,0},{2,3},{3,2},{4,5},{5,4},{6,7},{7,6},{8,9},{9,8},{10,11... | collective-permute-start | bytes 8257544 | tf_op jit(solution)/shard_map/ppermute | solution.py:135
  58.7 3.8 %collective-permute-start.2 = (f32[1024,128]{1,0:T(8,128)S(1)}, f32[1024,128]{1,0:T(8,128)S(1)}, u32[]{:S(2)}, u32[]{:S(2)}) collective-permute-start(f32[1024,128]{1,0:T(8,128)S(1)} %get-tuple-element.16), channel_id=1, source_target_pairs={{0,1},{1,0},{2,3},{3,2},{4,5},{5,4},{6,7},{7,6},{8,9},{9,8},{10,11... | collective-permute-start | bytes 1572872 | tf_op jit(solution)/shard_map/ppermute | solution.py:140
  63.4 37.9 %all-to-all-start.3 = ((f32[8,128,128]{2,1,0:T(8,128)}), f32[8,128,128]{2,1,0:T(8,128)S(1)}, u32[]{:S(2)}, u32[]{:S(2)}) async-start(f32[8,128,128]{2,1,0:T(8,128)} %bitcast.5), calls=%async_computation.3 | async-start | bytes 1048576 | tf_op jit(solution)/shard_map/all_to_all | solution.py:21
  89.0 2.0 %copy-start.1 = (bf16[512,3584]{1,0:T(8,128)(2,1)S(1)}, bf16[512,3584]{1,0:T(8,128)(2,1)}, u32[]{:S(2)}) copy-start(bf16[512,3584]{1,0:T(8,128)(2,1)} %all-gather.2.cloned.1.call-done.grads_ref) | copy-start | bytes 11010052
  91.0 1.8 copy-start.2
  101.3 16.6 %all-to-all-start = ((bf16[8,64,768]{2,1,0:T(8,128)(2,1)}), bf16[8,64,768]{2,1,0:T(8,128)(2,1)S(1)}, u32[]{:S(2)}, u32[]{:S(2)}) async-start(bf16[8,64,768]{2,1,0:T(8,128)(2,1)} %bitcast.1), calls=%async_computation | async-start | bytes 1572864 | tf_op jit(solution)/shard_map/all_to_all | solution.py:21
  119.2 36.5 %all-to-all-start.4 = ((bf16[32,128,128]{2,1,0:T(8,128)(2,1)}), bf16[32,128,128]{2,1,0:T(8,128)(2,1)S(1)}, u32[]{:S(2)}, u32[]{:S(2)}) async-start(bf16[32,128,128]{2,1,0:T(8,128)(2,1)} %broadcast_in_dim.22), calls=%async_computation.4 | async-start | bytes 2097152 | tf_op jit(solution)/shard_map/all_to_all | solution.py:21
  127.6 3.1 %collective-permute-start.1 = (bf16[64,384]{1,0:T(8,128)(2,1)S(1)}, bf16[64,384]{1,0:T(8,128)(2,1)S(1)}, u32[]{:S(2)}, u32[]{:S(2)}) collective-permute-start(bf16[64,384]{1,0:T(8,128)(2,1)S(1)} %slice.9), channel_id=1, source_target_pairs={{0,1},{1,0},{2,3},{3,2},{4,5},{5,4},{6,7},{7,6},{8,9},{9,8},{10,11... | collective-permute-start | bytes 147464 | tf_op jit(solution)/shard_map/ppermute | solution.py:150
  156.6 13.8 %all-to-all-start.1 = ((bf16[8,128,384]{2,1,0:T(8,128)(2,1)}), bf16[8,128,384]{2,1,0:T(8,128)(2,1)S(1)}, u32[]{:S(2)}, u32[]{:S(2)}) async-start(bf16[8,128,384]{2,1,0:T(8,128)(2,1)} %broadcast_in_dim.8), calls=%async_computation.1 | async-start | bytes 1572864 | tf_op jit(solution)/shard_map/all_to_all | solution.py:21
  160.3 4.5 %collective-permute-start.3 = (bf16[8,4,128,128]{3,2,1,0:T(8,128)(2,1)S(1)}, bf16[8,4,128,128]{3,2,1,0:T(8,128)(2,1)S(1)}, u32[]{:S(2)}, u32[]{:S(2)}) collective-permute-start(bf16[8,4,128,128]{3,2,1,0:T(8,128)(2,1)S(1)} %bitcast.17), channel_id=1, source_target_pairs={{0,1},{1,0},{2,3},{3,2},{4,5},{5,4},{6,7},{7,6},{8,9},{9,8},{10,11... | collective-permute-start | bytes 3145736 | tf_op jit(solution)/shard_map/ppermute | solution.py:144
Sparse Core Ops, SparseCore 0:
  29.4 59.5 all-gather.1

commit v3 on v0

v3 whole, which is shorter than its diff:
```python
import jax
import jax.numpy as jnp
from jax import lax
from jax.experimental import pallas as pl
from jax.experimental.pallas import tpu as pltpu
from jax.sharding import Mesh, PartitionSpec as P

SEQS = 4
SWAP = [(0, 1), (1, 0)]
GRP = ("x", "zl")
F32 = jnp.float32
BF16 = jnp.bfloat16
VMEM = pl.BlockSpec(memory_space=pltpu.VMEM)
SMEM = pl.BlockSpec(memory_space=pltpu.SMEM)
PARAMS = pltpu.CompilerParams(vmem_limit_bytes=32 * 1024 * 1024)


def dot(a, b):
    return jnp.dot(a, b, preferred_element_type=F32)


def exchange(pieces, axis):
    return lax.all_to_all(pieces, axis, 0, 0)


def spread(piece, axis, n):
    return exchange(jnp.broadcast_to(piece[None], (n,) + piece.shape), axis)


def shift(value, axis, n, by):
    return lax.ppermute(value, axis, [(i, (i + by) % n) for i in range(n)])


def grad_kernel(grads_ref, bases_ref, out_ref, rows_ref, sems):
    depth = 512
    copies = [
        pltpu.make_async_copy(grads_ref.at[:, pl.ds(depth * k, depth)], rows_ref.at[:, pl.ds(depth * k, depth)], sems.at[k])
        for k in range(7)
    ]
    for copy in copies:
        copy.start()
    total = None
    for k in range(7):
        copies[k].wait()
        part = dot(rows_ref[:, depth * k : depth * k + depth], bases_ref[depth * k : depth * k + depth, :256])
        total = part if k == 0 else total + part
    out_ref[:, :256] = total.astype(BF16)
    for n in (256, 512):
        out_ref[:, n : n + 256] = dot(rows_ref[...], bases_ref[:, n : n + 256]).astype(BF16)


def project_grads(grads, bases):
    return pl.pallas_call(
        grad_kernel,
        in_specs=[pl.BlockSpec(memory_space=pltpu.HBM), VMEM],
        out_specs=VMEM,
        out_shape=jax.ShapeDtypeStruct((512, 768), BF16),
        scratch_shapes=[pltpu.VMEM((512, 3584), BF16), pltpu.SemaphoreType.DMA((7,))],
        compiler_params=PARAMS,
        name="project_grads",
    )(grads, bases)


def pieces_kernel(index_ref, acts_ref, weights_ref, out_ref):
    for t in range(2):
        share = acts_ref[pl.ds(pl.multiple_of(512 * t + 64 * index_ref[0], 64), 64), :]
        for q in range(4):
            out_ref[4 * t + q, :64, :] = share
            out_ref[4 * t + q, 64:192, :] = weights_ref[:, 256 * q : 256 * q + 128]
            out_ref[4 * t + q, 192:320, :] = weights_ref[:, 256 * q + 128 : 256 * q + 256]


def make_pieces(index, acts, weights):
    return pl.pallas_call(
        pieces_kernel,
        in_specs=[SMEM, VMEM, VMEM],
        out_specs=VMEM,
        out_shape=jax.ShapeDtypeStruct((8, 320, 128), BF16),
        compiler_params=PARAMS,
        name="make_pieces",
    )(index, acts, weights)


def act_kernel(acts_ref, pieces_ref, out_ref):
    total = None
    for y in range(0, 8, 2):
        acts = jnp.concatenate([acts_ref[:, y].reshape(512, 128), acts_ref[:, y + 1].reshape(512, 128)], axis=1)
        rows = [jnp.concatenate([pieces_ref[y + i, 64:192, :], pieces_ref[y + i, 192:, :]], axis=1) for i in range(2)]
        part = dot(acts, jnp.concatenate(rows, axis=0))
        total = part if y == 0 else total + part
    out_ref[...] = total


def project_acts(acts, pieces):
    return pl.pallas_call(
        act_kernel,
        in_specs=[VMEM, VMEM],
        out_specs=VMEM,
        out_shape=jax.ShapeDtypeStruct((512, 256), F32),
        compiler_params=PARAMS,
        name="project_acts",
    )(acts, pieces)


def fit_kernel(grad_ref, act_ref, out_ref, held_ref, sum_ref, in_sems, out_sems):
    loads = [pltpu.make_async_copy(act_ref.at[y], held_ref.at[y], in_sems.at[y]) for y in range(8)]
    for q in range(4):
        loads[q].start()
        loads[4 + q].start()
    grads = [grad_ref[256 * s : 256 * s + 256, :].T for s in range(SEQS)]
    stores = []
    for q in range(4):
        total = None
        for t in range(2):
            loads[4 * t + q].wait()
            for half in range(2):
                rows = []
                for y in range(2):
                    for parity in range(2):
                        for z in range(4):
                            at = 256 * half + 128 * y + 32 * z + 16 * parity
                            rows.append(held_ref[4 * t + q, at : at + 16, :])
                block = dot(grads[2 * t + half], jnp.concatenate(rows, axis=0))
                total = block * block if total is None else total + block * block
        sum_ref[q] = total * (1.0 / SEQS)
        store = pltpu.make_async_copy(sum_ref.at[q], out_ref.at[:, pl.ds(256 * q, 256)], out_sems.at[q])
        store.start()
        stores.append(store)
    for store in stores:
        store.wait()


def fit(grad, act):
    return pl.pallas_call(
        fit_kernel,
        in_specs=[VMEM, pl.BlockSpec(memory_space=pltpu.HBM)],
        out_specs=pl.BlockSpec(memory_space=pltpu.HBM),
        out_shape=jax.ShapeDtypeStruct((384, 1024), F32),
        scratch_shapes=[
            pltpu.VMEM((8, 512, 256), BF16),
            pltpu.VMEM((4, 384, 256), F32),
            pltpu.SemaphoreType.DMA((8,)),
            pltpu.SemaphoreType.DMA((4,)),
        ],
        compiler_params=PARAMS,
        name="fit_blocks",
    )(grad, act)


def local(out_grads, in_acts, basis_out, basis_in):
    core = lax.axis_index("core")
    group = lax.axis_index(GRP).astype(jnp.int32).reshape(1)

    pieces = make_pieces(group, in_acts, basis_in)
    pieces, out_grads = lax.optimization_barrier((pieces, out_grads))
    pieces = exchange(pieces, "y")

    grads = lax.all_gather(out_grads, "zh", axis=0, tiled=True)
    grads, pieces, basis_out = lax.optimization_barrier((grads, pieces, basis_out))
    grads = lax.all_gather(grads, "y", axis=0, tiled=True)
    basis_other = lax.ppermute(basis_out, "core", SWAP)
    bases = jnp.concatenate([basis_out, basis_other], axis=1)

    acts = spread(pieces[:, :64], GRP, 8)
    acts, bases = lax.optimization_barrier((acts, bases))
    act = project_acts(acts, pieces)
    act = jnp.sum(exchange(act.reshape(8, 64, 256), ("zh", "core")), axis=0).astype(BF16)
    act = spread(act, ("zh", "core"), 8).reshape(512, 256)
    partial = project_grads(grads, bases)
    _, partial = lax.optimization_barrier((act, partial))
    act = lax.all_gather(act, "y", axis=0)

    parts = exchange(partial.reshape(8, 64, 768), GRP)
    both = jnp.sum(parts.astype(F32), axis=0).astype(BF16)
    own, rest = both[:, :384], both[:, 384:]
    pair = jnp.stack([jnp.where(core == 0, own, rest), jnp.where(core == 0, rest, own)])
    pair = jnp.broadcast_to(pair[None], (8, 2, 64, 384)).reshape(16, 64, 384)
    grad = exchange(pair, GRP + ("core",)).reshape(1024, 384)

    return fit(grad, act)


def solution(mesh):
    fine = Mesh(mesh.devices.reshape(4, 2, 8, 4, 2), ("x", "zl", "y", "zh", "core"))
    col = ("y", "zh", "core")
    return jax.shard_map(
        local,
        mesh=fine,
        in_specs=(P(col, GRP), P(None, col), P(GRP, col), P(col, GRP)),
        out_specs=P(col, GRP),
        check_vma=False,
    )
```

time: 460 us -> 162 us (0.35)
  the two profiles are of different devices: /device:TPU:6 before, /device:TPU:1 now
where the time goes in v3:
time: 162 us; the launch traced here: 161 us
  blocking collectives  59.3 us (37%)
  waiting for transfers between devices  33.5 us (21%)
  starting transfers between devices  29.1 us (18%)
  between operations  13.5 us (8%)
  local copies, waits for them, and re-layouts  10.3 us (6%)
  Pallas kernels  10.1 us (6%)
  other arithmetic  5.63 us (3%)
    all_to_all x2, blocking collectives, exchange(): return lax.all_to_all(pieces, axis, 0, 0)  39 us
    all_to_all x4, waiting for transfers between devices, exchange(): return lax.all_to_all(pieces, axis, 0, 0)  31.8 us
    all_to_all x4, starting transfers between devices, exchange(): return lax.all_to_all(pieces, axis, 0, 0)  23.9 us
    all_gather x1, blocking collectives, local(): grads = lax.all_gather(out_grads, 'zh', axis=0, tiled=True)  20.3 us
    unnamed x10, local copies, waits for them, and re-layouts  8.08 us
    concatenate x1, other arithmetic, local(): bases = jnp.concatenate([basis_out, basis_other], axis=1)  5.45 us
    pallas_call x1, Pallas kernels, project_grads(): pl.pallas_call(grad_kernel, in_specs=[pl.BlockSpec(memory_space=pltpu.HBM...  5.36 us
    ppermute x1, starting transfers between devices, local(): basis_other = lax.ppermute(basis_out, 'core', SWAP)  5.2 us
  transfers between devices with their start and end apart: 7, of which 4 were waited for; matrix products, arithmetic and copies ran while one was open for 5% of the time, Pallas kernels for 4%

profile of v3, /device:TPU:1, one launch (start us, length us, event | category | flops | bytes accessed | tf_op | source)
XLA Modules:
  0.0 161.5 jit_solution(2402366771053193954)
XLA Ops:
  6.5 0.9 copy-done.3
  7.5 0.9 copy-done.4
  8.4 0.9 make_pieces.1
  9.4 7.7 %all-to-all-start = ((bf16[8,320,128]{2,1,0:T(8,128)(2,1)}), bf16[8,320,128]{2,1,0:T(8,128)(2,1)S(1)}, u32[]{:S(2)}, u32[]{:S(2)}) async-start(bf16[8,320,128]{2,1,0:T(8,128)(2,1)} %make_pieces.1), calls=%async_computation | async-start | bytes 1310720 | tf_op jit(solution)/shard_map/all_to_all | solution.py:23
  17.0 0.0 all-gather.3.cloned.1.call-start
  17.1 20.3 %all_gather.9 = bf16[64,3584]{1,0:T(8,128)(2,1)} all-gather(bf16[16,3584]{1,0:T(8,128)(2,1)} %param.4), channel_id=1, replica_groups=mesh['x'=4,'zl'=2,'y'=8,'zh'=4,'core'=2] {'zh'}, dimensions={0}, use_global_device_ids=true | all-gather | bytes 573440 | tf_op jit(solution)/shard_map/all_gather | solution.py:158
  37.3 0.0 all-to-all-done.pieces_ref
  37.3 0.0 all-gather.3.cloned.1.call-update
  37.3 5.2 %collective-permute-start = (bf16[3584,384]{1,0:T(8,128)(2,1)}, bf16[3584,384]{1,0:T(8,128)(2,1)}, u32[]{:S(2)}, u32[]{:S(2)}) collective-permute-start(bf16[3584,384]{1,0:T(8,128)(2,1)} %param.6), channel_id=1, source_target_pairs={{0,1},{1,0},{2,3},{3,2},{4,5},{5,4},{6,7},{7,6},{8,9},{9,8},{10,11... | collective-permute-start | bytes 8257544 | tf_op jit(solution)/shard_map/ppermute | solution.py:161
  42.6 1.2 broadcast_in_dim.6
  43.8 5.3 %all-to-all-start.1 = ((bf16[8,8,64,128]{3,2,1,0:T(8,128)(2,1)}), bf16[8,8,64,128]{3,2,1,0:T(8,128)(2,1)S(1)}, u32[]{:S(2)}, u32[]{:S(2)}) async-start(bf16[8,8,64,128]{3,2,1,0:T(8,128)(2,1)} %broadcast_in_dim.6), calls=%async_computation.1 | async-start | bytes 2097152 | tf_op jit(solution)/shard_map/all_to_all | solution.py:23
  49.1 0.0 all-gather.5.cloned.1.call-start
  49.2 0.0 collective-permute-done
  49.2 5.4 %pad_maximum_fusion.bases_ref = bf16[3584,768]{1,0:T(8,128)(2,1)} fusion(bf16[3584,384]{1,0:T(8,128)(2,1)} %collective-permute-done, bf16[3584,384]{1,0:T(8,128)(2,1)} %param.6), kind=kLoop, calls=%fused_computation | loop fusion | flops 11010048 | bytes 11010048 | tf_op jit(solution)/shard_map/concatenate | solution.py:162
  54.6 10.1 %all-to-all-done.1.acts_ref = bf16[8,8,64,128]{3,2,1,0:T(8,128)(2,1)S(1)} async-done(((bf16[8,8,64,128]{3,2,1,0:T(8,128)(2,1)}), bf16[8,8,64,128]{3,2,1,0:T(8,128)(2,1)S(1)}, u32[]{:S(2)}, u32[]{:S(2)}) %all-to-all-start.1) | async-done | bytes 1048608 | tf_op jit(solution)/shard_map/all_to_all | solution.py:23
  64.7 0.4 project_acts.1
  65.2 24.4 %all_to_all.30 = f32[8,64,256]{2,1,0:T(8,128)S(1)} all-to-all(f32[8,64,256]{2,1,0:T(8,128)S(1)} %bitcast.11), channel_id=1, replica_groups=mesh['x'=4,'zl'=2,'y'=8,'zh'=4,'core'=2] {'zh','core'}, dimensions={0} | all-to-all | bytes 1048576 | tf_op jit(solution)/shard_map/all_to_all | solution.py:23
  89.6 14.6 %all_to_all.31 = bf16[8,64,256]{2,1,0:T(8,128)(2,1)} all-to-all(bf16[8,64,256]{2,1,0:T(8,128)(2,1)S(1)} %broadcast_in_dim.8), channel_id=1, replica_groups=mesh['x'=4,'zl'=2,'y'=8,'zh'=4,'core'=2] {'zh','core'}, dimensions={0} | all-to-all | bytes 524288 | tf_op jit(solution)/shard_map/all_to_all | solution.py:23
  104.2 0.0 all-gather.5.cloned.1.call-update
  104.3 0.0 all-gather.3.cloned.1.call-done.grads_ref
  104.3 2.6 %copy-done = bf16[3584,768]{1,0:T(8,128)(2,1)S(1)} copy-done((bf16[3584,768]{1,0:T(8,128)(2,1)S(1)}, bf16[3584,768]{1,0:T(8,128)(2,1)}, u32[]{:S(2)}) %copy-start) | copy-done | bytes 5505048
  106.8 2.0 %copy-done.1 = bf16[512,3584]{1,0:T(8,128)(2,1)S(1)} copy-done((bf16[512,3584]{1,0:T(8,128)(2,1)S(1)}, bf16[512,3584]{1,0:T(8,128)(2,1)}, u32[]{:S(2)}) %copy-start.1) | copy-done | bytes 3670040
  108.9 5.4 %project_grads.1 = bf16[512,768]{1,0:T(8,128)(2,1)} custom-call(bf16[512,3584]{1,0:T(8,128)(2,1)S(1)} %copy-done.1, bf16[3584,768]{1,0:T(8,128)(2,1)S(1)} %copy-done), custom_call_target="tpu_custom_call" | custom-call | tf_op jit(solution)/shard_map/project_grads/pallas_call | solution.py:53
  114.2 3.8 %all-to-all-start.2 = ((bf16[8,64,768]{2,1,0:T(8,128)(2,1)}), bf16[8,64,768]{2,1,0:T(8,128)(2,1)S(1)}, u32[]{:S(2)}, u32[]{:S(2)}) async-start(bf16[8,64,768]{2,1,0:T(8,128)(2,1)} %bitcast.1), calls=%async_computation.2 | async-start | bytes 1572864 | tf_op jit(solution)/shard_map/all_to_all | solution.py:23
  118.1 10.3 %all-to-all-done.2 = bf16[8,64,768]{2,1,0:T(8,128)(2,1)S(1)} async-done(((bf16[8,64,768]{2,1,0:T(8,128)(2,1)}), bf16[8,64,768]{2,1,0:T(8,128)(2,1)S(1)}, u32[]{:S(2)}, u32[]{:S(2)}) %all-to-all-start.2) | async-done | bytes 786464 | tf_op jit(solution)/shard_map/all_to_all | solution.py:23
  128.4 0.1 reduce_sum.21
  128.5 1.0 broadcast_in_dim.7
  129.5 7.0 %all-to-all-start.3 = ((bf16[16,64,384]{2,1,0:T(8,128)(2,1)}), bf16[16,64,384]{2,1,0:T(8,128)(2,1)S(1)}, u32[]{:S(2)}, u32[]{:S(2)}) async-start(bf16[16,64,384]{2,1,0:T(8,128)(2,1)} %bitcast.4), calls=%async_computation.3 | async-start | bytes 1572864 | tf_op jit(solution)/shard_map/all_to_all | solution.py:23
  136.6 1.7 %all-gather.5.cloned.1.call-done.act_ref = bf16[8,512,256]{2,1,0:T(8,128)(2,1)} async-done(((bf16[1,512,256]{2,1,0:T(8,128)(2,1)}), bf16[8,512,256]{2,1,0:T(8,128)(2,1)}) %all-gather.5.cloned.1.call-update) | async-done | bytes 2097168 | tf_op jit(solution)/shard_map/all_gather | solution.py:171
  138.2 11.4 %all-to-all-done.3 = bf16[16,64,384]{2,1,0:T(8,128)(2,1)S(1)} async-done(((bf16[16,64,384]{2,1,0:T(8,128)(2,1)}), bf16[16,64,384]{2,1,0:T(8,128)(2,1)S(1)}, u32[]{:S(2)}, u32[]{:S(2)}) %all-to-all-start.3) | async-done | bytes 786464 | tf_op jit(solution)/shard_map/all_to_all | solution.py:23
  149.6 1.6 copy-done.2
  151.2 3.4 %fit_blocks.1 = f32[384,1024]{1,0:T(8,128)} custom-call(bf16[1024,384]{1,0:T(8,128)(2,1)S(1)} %bitcast.10, bf16[8,512,256]{2,1,0:T(8,128)(2,1)S(1)} %copy-done.2), custom_call_target="tpu_custom_call" | custom-call | tf_op jit(solution)/shard_map/fit_blocks/pallas_call | solution.py:134
  (10 shorter events, 0.1 us)
Async XLA Ops:
  6.5 0.9 copy-start.3
  7.5 0.9 copy-start.4
  9.4 28.0 %all-to-all-start = ((bf16[8,320,128]{2,1,0:T(8,128)(2,1)}), bf16[8,320,128]{2,1,0:T(8,128)(2,1)S(1)}, u32[]{:S(2)}, u32[]{:S(2)}) async-start(bf16[8,320,128]{2,1,0:T(8,128)(2,1)} %make_pieces.1), calls=%async_computation | async-start | bytes 1310720 | tf_op jit(solution)/shard_map/all_to_all | solution.py:23
  17.0 87.3 %all-gather.3.cloned.1.call-start = ((), (), s32[]{:S(2)}) async-start(), calls=%async_computation.6 | async-start | bytes 4128768 | tf_op jit(solution)/shard_map/all_gather | solution.py:160
  37.3 11.8 %collective-permute-start = (bf16[3584,384]{1,0:T(8,128)(2,1)}, bf16[3584,384]{1,0:T(8,128)(2,1)}, u32[]{:S(2)}, u32[]{:S(2)}) collective-permute-start(bf16[3584,384]{1,0:T(8,128)(2,1)} %param.6), channel_id=1, source_target_pairs={{0,1},{1,0},{2,3},{3,2},{4,5},{5,4},{6,7},{7,6},{8,9},{9,8},{10,11... | collective-permute-start | bytes 8257544 | tf_op jit(solution)/shard_map/ppermute | solution.py:161
  43.8 20.9 %all-to-all-start.1 = ((bf16[8,8,64,128]{3,2,1,0:T(8,128)(2,1)}), bf16[8,8,64,128]{3,2,1,0:T(8,128)(2,1)S(1)}, u32[]{:S(2)}, u32[]{:S(2)}) async-start(bf16[8,8,64,128]{3,2,1,0:T(8,128)(2,1)} %broadcast_in_dim.6), calls=%async_computation.1 | async-start | bytes 2097152 | tf_op jit(solution)/shard_map/all_to_all | solution.py:23
  49.1 89.1 %all-gather.5.cloned.1.call-start = ((), (), s32[]{:S(2)}) async-start(), calls=%async_computation.7 | async-start | bytes 2359296 | tf_op jit(solution)/shard_map/all_gather | solution.py:171
  104.3 2.6 %copy-start = (bf16[3584,768]{1,0:T(8,128)(2,1)S(1)}, bf16[3584,768]{1,0:T(8,128)(2,1)}, u32[]{:S(2)}) copy-start(bf16[3584,768]{1,0:T(8,128)(2,1)} %pad_maximum_fusion.bases_ref) | copy-start | bytes 16515076
  106.8 2.0 %copy-start.1 = (bf16[512,3584]{1,0:T(8,128)(2,1)S(1)}, bf16[512,3584]{1,0:T(8,128)(2,1)}, u32[]{:S(2)}) copy-start(bf16[512,3584]{1,0:T(8,128)(2,1)} %all-gather.3.cloned.1.call-done.grads_ref) | copy-start | bytes 11010052
  114.2 14.1 %all-to-all-start.2 = ((bf16[8,64,768]{2,1,0:T(8,128)(2,1)}), bf16[8,64,768]{2,1,0:T(8,128)(2,1)S(1)}, u32[]{:S(2)}, u32[]{:S(2)}) async-start(bf16[8,64,768]{2,1,0:T(8,128)(2,1)} %bitcast.1), calls=%async_computation.2 | async-start | bytes 1572864 | tf_op jit(solution)/shard_map/all_to_all | solution.py:23
  129.5 20.1 %all-to-all-start.3 = ((bf16[16,64,384]{2,1,0:T(8,128)(2,1)}), bf16[16,64,384]{2,1,0:T(8,128)(2,1)S(1)}, u32[]{:S(2)}, u32[]{:S(2)}) async-start(bf16[16,64,384]{2,1,0:T(8,128)(2,1)} %bitcast.4), calls=%async_computation.3 | async-start | bytes 1572864 | tf_op jit(solution)/shard_map/all_to_all | solution.py:23
  149.6 1.6 copy-start.2
Sparse Core Ops, SparseCore 0:
  37.5 54.1 all-gather.2
  104.4 33.7 all-gather.4

commit v4 on v3

v4 whole, which is shorter than its diff:
```python
import jax
import jax.numpy as jnp
from jax import lax
from jax.experimental import pallas as pl
from jax.experimental.pallas import tpu as pltpu
from jax.sharding import Mesh, PartitionSpec as P

SEQS = 4
SWAP = [(0, 1), (1, 0)]
GRP = ("x", "zl")
F32 = jnp.float32
BF16 = jnp.bfloat16
VMEM = pl.BlockSpec(memory_space=pltpu.VMEM)
SMEM = pl.BlockSpec(memory_space=pltpu.SMEM)
HBM = pl.BlockSpec(memory_space=pltpu.HBM)
ALONE = pltpu.CompilerParams(vmem_limit_bytes=60 * 1024 * 1024)
PARAMS = pltpu.CompilerParams(vmem_limit_bytes=32 * 1024 * 1024)


def dot(a, b):
    return jnp.dot(a, b, preferred_element_type=F32)


def exchange(pieces, axis):
    return lax.all_to_all(pieces, axis, 0, 0)


def spread(piece, axis, n):
    return exchange(jnp.broadcast_to(piece[None], (n,) + piece.shape), axis)


def shift(value, axis, n, by):
    return lax.ppermute(value, axis, [(i, (i + by) % n) for i in range(n)])


def grad_kernel(grads_ref, bases_ref, out_ref, rows_ref, held_ref, sems):
    rows = [pltpu.make_async_copy(grads_ref.at[pl.ds(128 * m, 128)], rows_ref.at[pl.ds(128 * m, 128)], sems.at[m]) for m in range(4)]
    tiles = [pltpu.make_async_copy(bases_ref.at[n], held_ref.at[n], sems.at[4 + n]) for n in range(3)]
    for copy in [tiles[0]] + rows + tiles[1:]:
        copy.start()
    tiles[0].wait()
    for m in range(4):
        rows[m].wait()
        at = slice(128 * m, 128 * m + 128)
        out_ref[at, :256] = dot(rows_ref[at, :], held_ref[0]).astype(BF16)
    for n in (1, 2):
        tiles[n].wait()
        out_ref[:, 256 * n : 256 * n + 256] = dot(rows_ref[...], held_ref[n]).astype(BF16)


def project_grads(grads, bases):
    return pl.pallas_call(
        grad_kernel,
        in_specs=[HBM, HBM],
        out_specs=VMEM,
        out_shape=jax.ShapeDtypeStruct((512, 768), BF16),
        scratch_shapes=[
            pltpu.VMEM((512, 3584), BF16),
            pltpu.VMEM((3, 3584, 256), BF16),
            pltpu.SemaphoreType.DMA((7,)),
        ],
        compiler_params=ALONE,
        name="project_grads",
    )(grads, bases)


def pieces_kernel(index_ref, acts_ref, weights_ref, out_ref, sems):
    copies = []
    for y in range(8):
        t, q = y // 4, y % 4
        share = acts_ref.at[pl.ds(pl.multiple_of(512 * t + 64 * index_ref[0], 64), 64)]
        copies.append(pltpu.make_async_copy(share, out_ref.at[y, pl.ds(0, 64)], sems.at[y]))
        for c in range(2):
            tile = weights_ref.at[:, pl.ds(256 * q + 128 * c, 128)]
            copies.append(pltpu.make_async_copy(tile, out_ref.at[y, pl.ds(64 + 128 * c, 128)], sems.at[8 + 2 * y + c]))
    for copy in copies:
        copy.start()
    for copy in copies:
        copy.wait()


def make_pieces(index, acts, weights):
    return pl.pallas_call(
        pieces_kernel,
        in_specs=[SMEM, HBM, HBM],
        out_specs=VMEM,
        out_shape=jax.ShapeDtypeStruct((8, 320, 128), BF16),
        scratch_shapes=[pltpu.SemaphoreType.DMA((24,))],
        compiler_params=ALONE,
        name="make_pieces",
    )(index, acts, weights)


def act_kernel(acts_ref, pieces_ref, out_ref):
    total = None
    for y in range(0, 8, 2):
        acts = jnp.concatenate([acts_ref[:, y].reshape(512, 128), acts_ref[:, y + 1].reshape(512, 128)], axis=1)
        rows = [jnp.concatenate([pieces_ref[y + i, 64:192, :], pieces_ref[y + i, 192:, :]], axis=1) for i in range(2)]
        part = dot(acts, jnp.concatenate(rows, axis=0))
        total = part if y == 0 else total + part
    out_ref[...] = total


def project_acts(acts, pieces):
    return pl.pallas_call(
        act_kernel,
        in_specs=[VMEM, VMEM],
        out_specs=VMEM,
        out_shape=jax.ShapeDtypeStruct((512, 256), F32),
        compiler_params=PARAMS,
        name="project_acts",
    )(acts, pieces)


def fit_kernel(grad_ref, act_ref, out_ref, sum_ref, sems):
    grads = [grad_ref[256 * s : 256 * s + 256, :].T for s in range(SEQS)]
    stores = []
    for q in range(4):
        total = None
        for s in range(SEQS):
            block = dot(grads[s], act_ref[4 * (s // 2) + q, 256 * (s % 2) : 256 * (s % 2) + 256, :])
            total = block * block if total is None else total + block * block
        sum_ref[q] = total * (1.0 / SEQS)
        store = pltpu.make_async_copy(sum_ref.at[q], out_ref.at[:, pl.ds(256 * q, 256)], sems.at[q])
        store.start()
        stores.append(store)
    for store in stores:
        store.wait()


def fit(grad, act):
    return pl.pallas_call(
        fit_kernel,
        in_specs=[VMEM, VMEM],
        out_specs=HBM,
        out_shape=jax.ShapeDtypeStruct((384, 1024), F32),
        scratch_shapes=[pltpu.VMEM((4, 384, 256), F32), pltpu.SemaphoreType.DMA((4,))],
        compiler_params=PARAMS,
        name="fit_blocks",
    )(grad, act)


def local(out_grads, in_acts, basis_out, basis_in):
    core = lax.axis_index("core")
    group = lax.axis_index(GRP).astype(jnp.int32).reshape(1)

    pieces = make_pieces(group, in_acts, basis_in)
    pieces, out_grads = lax.optimization_barrier((pieces, out_grads))
    pieces = exchange(pieces, "y")

    grads = lax.all_gather(out_grads, "zh", axis=0, tiled=True)
    grads, pieces = lax.optimization_barrier((grads, pieces))
    grads = lax.all_gather(grads, "y", axis=0, tiled=True)
    basis_other = lax.ppermute(basis_out, "core", SWAP)
    middle = jnp.concatenate([basis_out[:, 256:], basis_other[:, :128]], axis=1)
    bases = jnp.stack([basis_out[:, :256], middle, basis_other[:, 128:]])

    acts = spread(pieces[:, :64], GRP, 8)
    acts, bases = lax.optimization_barrier((acts, bases))
    act = project_acts(acts, pieces)
    own = act.reshape(8, 64, 256)
    sums = exchange(own.astype(BF16), ("zh", "core")).astype(F32)
    index = lax.axis_index(("zh", "core"))
    mine = (jnp.arange(8) == index)[:, None, None]
    act = jnp.sum(jnp.where(mine, own, sums), axis=0).astype(BF16)
    act = spread(act, ("zh", "core"), 8).reshape(512, 256)
    partial = project_grads(grads, bases)
    _, partial = lax.optimization_barrier((act, partial))
    act = lax.all_gather(act, "y", axis=0)
    act = act.reshape(8, 4, 4, 2, 16, 256).transpose(0, 1, 3, 2, 4, 5).reshape(8, 512, 256)

    parts = exchange(partial.reshape(8, 64, 768), GRP)
    both = jnp.sum(parts.astype(F32), axis=0).astype(BF16)
    own, rest = both[:, :384], both[:, 384:]
    pair = jnp.stack([jnp.where(core == 0, own, rest), jnp.where(core == 0, rest, own)])
    pair = jnp.broadcast_to(pair[None], (8, 2, 64, 384)).reshape(16, 64, 384)
    grad = exchange(pair, GRP + ("core",)).reshape(1024, 384)

    return fit(grad, act)


def solution(mesh):
    fine = Mesh(mesh.devices.reshape(4, 2, 8, 4, 2), ("x", "zl", "y", "zh", "core"))
    col = ("y", "zh", "core")
    return jax.shard_map(
        local,
        mesh=fine,
        in_specs=(P(col, GRP), P(None, col), P(GRP, col), P(col, GRP)),
        out_specs=P(col, GRP),
        check_vma=False,
    )
```

time: 162 us -> 153 us (0.944)
  blocking collectives: 59.3 us -> 34.9 us
  starting transfers between devices: 29.1 us -> 37.8 us
  waiting for transfers between devices: 33.5 us -> 38.5 us
  Pallas kernels: 10.1 us -> 13.6 us
  local copies, waits for them, and re-layouts: 10.3 us -> 8.22 us
    all_to_all x2 -> x1, blocking collectives: 39 us -> 14.6 us  [exchange(): return lax.all_to_all(pieces, axis, 0, 0)]
    all_to_all x4 -> x5, starting transfers between devices: 23.9 us -> 32.7 us  [exchange(): return lax.all_to_all(pieces, axis, 0, 0)]
    unnamed x10 -> x0, local copies, waits for them, and re-layouts: 8.08 us -> none
    concatenate x1 -> x0, other arithmetic: 5.45 us -> none  [local(): bases = jnp.concatenate([basis_out, basis_other], axis=1)]
    another operation x0 -> x2, other arithmetic: none -> 4.81 us  [local(): bases = jnp.stack([basis_out[:, :256], middle, basis_other[:, 128:]])]
    all_to_all x4 -> x5, waiting for transfers between devices: 31.8 us -> 36.1 us  [exchange(): return lax.all_to_all(pieces, axis, 0, 0)]
    pallas_call x3, Pallas kernels: 9.68 us -> 13.2 us  [the longest x1 9.24 us: project_grads(): pl.pallas_call(grad_kernel, in_specs=[HBM, HBM], out_specs=VMEM, out_shap...]
    slice x0 -> x2, local copies, waits for them, and re-layouts: none -> 2.48 us  [local(): middle = jnp.concatenate([basis_out[:, 256:], basis_other[:, :128]], axis=1)]
  transfers between devices with their start and end apart: 7 -> 8, of which waited for: 4 -> 5; matrix products, arithmetic and copies ran while one was open for 5% -> 9% of each run, Pallas kernels for 4% -> 6%
where the time goes in v4:
time: 153 us; the launch traced here: 152 us
  waiting for transfers between devices  38.5 us (25%)
  starting transfers between devices  37.8 us (25%)
  blocking collectives  34.9 us (23%)
  Pallas kernels  13.6 us (9%)
  between operations  13.5 us (9%)
  local copies, waits for them, and re-layouts  8.22 us (5%)
  other arithmetic  5.81 us (4%)
    all_to_all x5, waiting for transfers between devices, exchange(): return lax.all_to_all(pieces, axis, 0, 0)  36.1 us
    all_to_all x5, starting transfers between devices, exchange(): return lax.all_to_all(pieces, axis, 0, 0)  32.7 us
    all_gather x1, blocking collectives, local(): grads = lax.all_gather(out_grads, 'zh', axis=0, tiled=True)  20.4 us
    all_to_all x1, blocking collectives, exchange(): return lax.all_to_all(pieces, axis, 0, 0)  14.6 us
    pallas_call x1, Pallas kernels, project_grads(): pl.pallas_call(grad_kernel, in_specs=[HBM, HBM], out_specs=VMEM, out_shap...  9.24 us
    ppermute x1, starting transfers between devices, local(): basis_other = lax.ppermute(basis_out, 'core', SWAP)  5.03 us
    another operation x2, other arithmetic, local(): bases = jnp.stack([basis_out[:, :256], middle, basis_other[:, 128:]])  4.81 us
  transfers between devices with their start and end apart: 8, of which 5 were waited for; matrix products, arithmetic and copies ran while one was open for 9% of the time, Pallas kernels for 6%

profile of v4, /device:TPU:1, one launch (start us, length us, event | category | flops | bytes accessed | tf_op | source)
XLA Modules:
  0.0 152.4 jit_solution(5654471934869980561)
XLA Ops:
  6.5 2.1 %make_pieces.1 = bf16[8,320,128]{2,1,0:T(8,128)(2,1)} custom-call(s32[1]{0:T(128)} %bitcast.index_ref, bf16[1024,128]{1,0:T(8,128)(2,1)} %acts_ref.1, bf16[128,1024]{1,0:T(8,128)(2,1)} %weights_ref.1), custom_call_target="tpu_custom_call" | custom-call | tf_op jit(solution)/shard_map/make_pieces/pallas_call | solution.py:83
  8.7 7.7 %all-to-all-start = ((bf16[8,320,128]{2,1,0:T(8,128)(2,1)}), bf16[8,320,128]{2,1,0:T(8,128)(2,1)S(1)}, u32[]{:S(2)}, u32[]{:S(2)}) async-start(bf16[8,320,128]{2,1,0:T(8,128)(2,1)} %make_pieces.1), calls=%async_computation | async-start | bytes 1310720 | tf_op jit(solution)/shard_map/all_to_all | solution.py:25
  16.4 0.0 all-gather.3.cloned.1.call-start
  16.4 20.4 %all_gather.9 = bf16[64,3584]{1,0:T(8,128)(2,1)} all-gather(bf16[16,3584]{1,0:T(8,128)(2,1)} %param.4), channel_id=1, replica_groups=mesh['x'=4,'zl'=2,'y'=8,'zh'=4,'core'=2] {'zh'}, dimensions={0}, use_global_device_ids=true | all-gather | bytes 573440 | tf_op jit(solution)/shard_map/all_gather | solution.py:151
  36.8 0.0 all-gather.3.cloned.1.call-update
  36.8 5.0 %collective-permute-start = (bf16[3584,384]{1,0:T(8,128)(2,1)}, bf16[3584,384]{1,0:T(8,128)(2,1)}, u32[]{:S(2)}, u32[]{:S(2)}) collective-permute-start(bf16[3584,384]{1,0:T(8,128)(2,1)} %param.6), channel_id=1, source_target_pairs={{0,1},{1,0},{2,3},{3,2},{4,5},{5,4},{6,7},{7,6},{8,9},{9,8},{10,11... | collective-permute-start | bytes 8257544 | tf_op jit(solution)/shard_map/ppermute | solution.py:154
  41.9 1.2 broadcast_in_dim.14
  43.1 5.5 %all-to-all-start.1 = ((bf16[8,8,64,128]{3,2,1,0:T(8,128)(2,1)}), bf16[8,8,64,128]{3,2,1,0:T(8,128)(2,1)S(1)}, u32[]{:S(2)}, u32[]{:S(2)}) async-start(bf16[8,8,64,128]{3,2,1,0:T(8,128)(2,1)} %broadcast_in_dim.14), calls=%async_computation.1 | async-start | bytes 2097152 | tf_op jit(solution)/shard_map/all_to_all | solution.py:25
  48.6 1.6 %slice_bitcast_fusion.1 = bf16[1,3584,256]{2,1,0:T(8,128)(2,1)S(1)} fusion(bf16[3584,384]{1,0:T(8,128)(2,1)} %param.6), kind=kLoop, calls=%fused_computation.3 | loop fusion | bytes 3670016 | tf_op jit(solution)/shard_map/stack | solution.py:156
  50.2 1.2 slice.23
  51.5 1.2 slice.28
  52.7 1.9 %slice_bitcast_fusion = (bf16[1,3584,256]{2,1,0:T(8,128)(2,1)S(1)}, bf16[1,3584,256]{2,1,0:T(8,128)(2,1)S(1)}) fusion(bf16[3584,384]{1,0:T(8,128)(2,1)} %collective-permute-done, bf16[3584,128]{1,0:T(8,128)(2,1)S(1)} %slice.28, bf16[3584,128]{1,0:T(8,128)(2,1)S(1)} %slice.23), kind=kLoop, calls=%fused_computation.1 | loop fusion | flops 3670016 | bytes 7340032 | tf_op jit(solution)/shard_map/stack | solution.py:156
  54.6 2.9 %pad_maximum_fusion.bases_ref = bf16[3,3584,256]{2,1,0:T(8,128)(2,1)} fusion(bf16[1,3584,256]{2,1,0:T(8,128)(2,1)S(1)} %get-tuple-element.19, bf16[1,3584,256]{2,1,0:T(8,128)(2,1)S(1)} %get-tuple-element.20, bf16[1,3584,256]{2,1,0:T(8,128)(2,1)S(1)} %slice_bitcast_fusion.1), kind=kLoop, calls=%fused_computation | loop fusion | flops 5505024 | bytes 11010048 | tf_op jit(solution)/shard_map/stack | solution.py:156
  57.5 6.7 %all-to-all-done.1.acts_ref = bf16[8,8,64,128]{3,2,1,0:T(8,128)(2,1)S(1)} async-done(((bf16[8,8,64,128]{3,2,1,0:T(8,128)(2,1)}), bf16[8,8,64,128]{3,2,1,0:T(8,128)(2,1)S(1)}, u32[]{:S(2)}, u32[]{:S(2)}) %all-to-all-start.1) | async-done | bytes 1048608 | tf_op jit(solution)/shard_map/all_to_all | solution.py:25
  64.2 0.4 project_acts.1
  64.6 0.7 bitcast_convert_fusion
  65.3 8.6 %all-to-all-start.4 = ((bf16[8,64,256]{2,1,0:T(8,128)(2,1)}), bf16[8,64,256]{2,1,0:T(8,128)(2,1)S(1)}, u32[]{:S(2)}, u32[]{:S(2)}) async-start(bf16[8,64,256]{2,1,0:T(8,128)(2,1)} %bitcast_convert_fusion), calls=%async_computation.4 | async-start | bytes 524288 | tf_op jit(solution)/shard_map/all_to_all | solution.py:25
  74.0 10.4 %all-to-all-done.4 = bf16[8,64,256]{2,1,0:T(8,128)(2,1)S(1)} async-done(((bf16[8,64,256]{2,1,0:T(8,128)(2,1)}), bf16[8,64,256]{2,1,0:T(8,128)(2,1)S(1)}, u32[]{:S(2)}, u32[]{:S(2)}) %all-to-all-start.4) | async-done | bytes 262176 | tf_op jit(solution)/shard_map/all_to_all | solution.py:25
  84.4 0.1 select_reduce_fusion
  84.5 14.6 %all_to_all.30 = bf16[8,64,256]{2,1,0:T(8,128)(2,1)} all-to-all(bf16[8,64,256]{2,1,0:T(8,128)(2,1)S(1)} %broadcast_in_dim.17), channel_id=1, replica_groups=mesh['x'=4,'zl'=2,'y'=8,'zh'=4,'core'=2] {'zh','core'}, dimensions={0} | all-to-all | bytes 524288 | tf_op jit(solution)/shard_map/all_to_all | solution.py:25
  99.1 0.0 all-gather.5.cloned.1.call-update
  99.1 0.0 all-gather.3.cloned.1.call-done.grads_ref
  99.1 9.2 %project_grads.1 = bf16[512,768]{1,0:T(8,128)(2,1)} custom-call(bf16[512,3584]{1,0:T(8,128)(2,1)} %all-gather.3.cloned.1.call-done.grads_ref, bf16[3,3584,256]{2,1,0:T(8,128)(2,1)} %pad_maximum_fusion.bases_ref), custom_call_target="tpu_custom_call" | custom-call | tf_op jit(solution)/shard_map/project_grads/pallas_call | solution.py:52
  108.4 3.8 %all-to-all-start.2 = ((bf16[8,64,768]{2,1,0:T(8,128)(2,1)}), bf16[8,64,768]{2,1,0:T(8,128)(2,1)S(1)}, u32[]{:S(2)}, u32[]{:S(2)}) async-start(bf16[8,64,768]{2,1,0:T(8,128)(2,1)} %bitcast.24), calls=%async_computation.2 | async-start | bytes 1572864 | tf_op jit(solution)/shard_map/all_to_all | solution.py:25
  112.2 10.3 %all-to-all-done.2 = bf16[8,64,768]{2,1,0:T(8,128)(2,1)S(1)} async-done(((bf16[8,64,768]{2,1,0:T(8,128)(2,1)}), bf16[8,64,768]{2,1,0:T(8,128)(2,1)S(1)}, u32[]{:S(2)}, u32[]{:S(2)}) %all-to-all-start.2) | async-done | bytes 786464 | tf_op jit(solution)/shard_map/all_to_all | solution.py:25
  122.4 0.1 reduce_sum.21
  122.6 1.0 broadcast_in_dim.15
  123.6 7.1 %all-to-all-start.3 = ((bf16[16,64,384]{2,1,0:T(8,128)(2,1)}), bf16[16,64,384]{2,1,0:T(8,128)(2,1)S(1)}, u32[]{:S(2)}, u32[]{:S(2)}) async-start(bf16[16,64,384]{2,1,0:T(8,128)(2,1)} %bitcast.7), calls=%async_computation.3 | async-start | bytes 1572864 | tf_op jit(solution)/shard_map/all_to_all | solution.py:25
  130.7 2.4 %all-gather.5.cloned.1.call-done = bf16[8,512,256]{2,1,0:T(8,128)(2,1)} async-done(((bf16[1,512,256]{2,1,0:T(8,128)(2,1)}), bf16[8,512,256]{2,1,0:T(8,128)(2,1)}) %all-gather.5.cloned.1.call-update) | async-done | bytes 2097168 | tf_op jit(solution)/shard_map/all_gather | solution.py:169
  133.0 1.9 %copy.6 = bf16[8,4,2,4,16,256]{5,4,3,2,1,0:T(8,128)(2,1)S(1)} copy(bf16[8,4,2,4,16,256]{5,4,2,3,1,0:T(8,128)(2,1)} %bitcast.25) | data formatting | bytes 4194304 | tf_op jit(solution)/shard_map/transpose | solution.py:170
  134.9 8.8 %all-to-all-done.3 = bf16[16,64,384]{2,1,0:T(8,128)(2,1)S(1)} async-done(((bf16[16,64,384]{2,1,0:T(8,128)(2,1)}), bf16[16,64,384]{2,1,0:T(8,128)(2,1)S(1)}, u32[]{:S(2)}, u32[]{:S(2)}) %all-to-all-start.3) | async-done | bytes 786464 | tf_op jit(solution)/shard_map/all_to_all | solution.py:25
  143.7 1.8 %fit_blocks.1 = f32[384,1024]{1,0:T(8,128)} custom-call(bf16[1024,384]{1,0:T(8,128)(2,1)S(1)} %bitcast.23, bf16[8,512,256]{2,1,0:T(8,128)(2,1)S(1)} %bitcast.21), custom_call_target="tpu_custom_call" | custom-call | tf_op jit(solution)/shard_map/fit_blocks/pallas_call | solution.py:132
  (8 shorter events, 0.1 us)
Async XLA Ops:
  8.7 28.1 %all-to-all-start = ((bf16[8,320,128]{2,1,0:T(8,128)(2,1)}), bf16[8,320,128]{2,1,0:T(8,128)(2,1)S(1)}, u32[]{:S(2)}, u32[]{:S(2)}) async-start(bf16[8,320,128]{2,1,0:T(8,128)(2,1)} %make_pieces.1), calls=%async_computation | async-start | bytes 1310720 | tf_op jit(solution)/shard_map/all_to_all | solution.py:25
  16.4 82.8 %all-gather.3.cloned.1.call-start = ((), (), s32[]{:S(2)}) async-start(), calls=%async_computation.6 | async-start | bytes 4128768 | tf_op jit(solution)/shard_map/all_gather | solution.py:153
  36.8 14.7 %collective-permute-start = (bf16[3584,384]{1,0:T(8,128)(2,1)}, bf16[3584,384]{1,0:T(8,128)(2,1)}, u32[]{:S(2)}, u32[]{:S(2)}) collective-permute-start(bf16[3584,384]{1,0:T(8,128)(2,1)} %param.6), channel_id=1, source_target_pairs={{0,1},{1,0},{2,3},{3,2},{4,5},{5,4},{6,7},{7,6},{8,9},{9,8},{10,11... | collective-permute-start | bytes 8257544 | tf_op jit(solution)/shard_map/ppermute | solution.py:154
  43.1 21.1 %all-to-all-start.1 = ((bf16[8,8,64,128]{3,2,1,0:T(8,128)(2,1)}), bf16[8,8,64,128]{3,2,1,0:T(8,128)(2,1)S(1)}, u32[]{:S(2)}, u32[]{:S(2)}) async-start(bf16[8,8,64,128]{3,2,1,0:T(8,128)(2,1)} %broadcast_in_dim.14), calls=%async_computation.1 | async-start | bytes 2097152 | tf_op jit(solution)/shard_map/all_to_all | solution.py:25
  65.3 19.0 %all-to-all-start.4 = ((bf16[8,64,256]{2,1,0:T(8,128)(2,1)}), bf16[8,64,256]{2,1,0:T(8,128)(2,1)S(1)}, u32[]{:S(2)}, u32[]{:S(2)}) async-start(bf16[8,64,256]{2,1,0:T(8,128)(2,1)} %bitcast_convert_fusion), calls=%async_computation.4 | async-start | bytes 524288 | tf_op jit(solution)/shard_map/all_to_all | solution.py:25
  74.0 59.0 %all-gather.5.cloned.1.call-start = ((), (), s32[]{:S(2)}) async-start(), calls=%async_computation.7 | async-start | bytes 2359296 | tf_op jit(solution)/shard_map/all_gather | solution.py:169
  108.4 14.1 %all-to-all-start.2 = ((bf16[8,64,768]{2,1,0:T(8,128)(2,1)}), bf16[8,64,768]{2,1,0:T(8,128)(2,1)S(1)}, u32[]{:S(2)}, u32[]{:S(2)}) async-start(bf16[8,64,768]{2,1,0:T(8,128)(2,1)} %bitcast.24), calls=%async_computation.2 | async-start | bytes 1572864 | tf_op jit(solution)/shard_map/all_to_all | solution.py:25
  123.6 20.1 %all-to-all-start.3 = ((bf16[16,64,384]{2,1,0:T(8,128)(2,1)}), bf16[16,64,384]{2,1,0:T(8,128)(2,1)S(1)}, u32[]{:S(2)}, u32[]{:S(2)}) async-start(bf16[16,64,384]{2,1,0:T(8,128)(2,1)} %bitcast.7), calls=%async_computation.3 | async-start | bytes 1572864 | tf_op jit(solution)/shard_map/all_to_all | solution.py:25
Sparse Core Ops, SparseCore 0:
  36.9 54.0 all-gather.2
  99.2 33.7 all-gather.4

commit v5 on v4

--- a/solution.py
+++ b/solution.py
@@ -33,33 +33,18 @@
     return lax.ppermute(value, axis, [(i, (i + by) % n) for i in range(n)])
 
 
-def grad_kernel(grads_ref, bases_ref, out_ref, rows_ref, held_ref, sems):
-    rows = [pltpu.make_async_copy(grads_ref.at[pl.ds(128 * m, 128)], rows_ref.at[pl.ds(128 * m, 128)], sems.at[m]) for m in range(4)]
-    tiles = [pltpu.make_async_copy(bases_ref.at[n], held_ref.at[n], sems.at[4 + n]) for n in range(3)]
-    for copy in [tiles[0]] + rows + tiles[1:]:
-        copy.start()
-    tiles[0].wait()
-    for m in range(4):
-        rows[m].wait()
-        at = slice(128 * m, 128 * m + 128)
-        out_ref[at, :256] = dot(rows_ref[at, :], held_ref[0]).astype(BF16)
-    for n in (1, 2):
-        tiles[n].wait()
-        out_ref[:, 256 * n : 256 * n + 256] = dot(rows_ref[...], held_ref[n]).astype(BF16)
+def grad_kernel(grads_ref, bases_ref, out_ref):
+    for n in range(3):
+        out_ref[:, 256 * n : 256 * n + 256] = dot(grads_ref[...], bases_ref[n]).astype(BF16)
 
 
 def project_grads(grads, bases):
     return pl.pallas_call(
         grad_kernel,
-        in_specs=[HBM, HBM],
+        in_specs=[VMEM, VMEM],
         out_specs=VMEM,
         out_shape=jax.ShapeDtypeStruct((512, 768), BF16),
-        scratch_shapes=[
-            pltpu.VMEM((512, 3584), BF16),
-            pltpu.VMEM((3, 3584, 256), BF16),
-            pltpu.SemaphoreType.DMA((7,)),
-        ],
-        compiler_params=ALONE,
+        compiler_params=PARAMS,
         name="project_grads",
     )(grads, bases)
 
@@ -91,25 +76,28 @@
     )(index, acts, weights)
 
 
-def act_kernel(acts_ref, pieces_ref, out_ref):
+def act_kernel(core_ref, acts_ref, pieces_ref, here_ref, there_ref):
     total = None
     for y in range(0, 8, 2):
         acts = jnp.concatenate([acts_ref[:, y].reshape(512, 128), acts_ref[:, y + 1].reshape(512, 128)], axis=1)
         rows = [jnp.concatenate([pieces_ref[y + i, 64:192, :], pieces_ref[y + i, 192:, :]], axis=1) for i in range(2)]
         part = dot(acts, jnp.concatenate(rows, axis=0))
         total = part if y == 0 else total + part
-    out_ref[...] = total
+    first = core_ref[0] == 0
+    here_ref[...] = jnp.where(first, total[:256], total[256:])
+    there_ref[...] = jnp.where(first, total[256:], total[:256])
 
 
-def project_acts(acts, pieces):
+def project_acts(core, acts, pieces):
+    half = jax.ShapeDtypeStruct((256, 256), F32)
     return pl.pallas_call(
         act_kernel,
-        in_specs=[VMEM, VMEM],
-        out_specs=VMEM,
-        out_shape=jax.ShapeDtypeStruct((512, 256), F32),
+        in_specs=[SMEM, VMEM, VMEM],
+        out_specs=[VMEM, VMEM],
+        out_shape=[half, half],
         compiler_params=PARAMS,
         name="project_acts",
-    )(acts, pieces)
+    )(core, acts, pieces)
 
 
 def fit_kernel(grad_ref, act_ref, out_ref, sum_ref, sems):
@@ -149,21 +137,21 @@
     pieces = exchange(pieces, "y")
 
     grads = lax.all_gather(out_grads, "zh", axis=0, tiled=True)
-    grads, pieces = lax.optimization_barrier((grads, pieces))
+    grads, pieces, basis_out = lax.optimization_barrier((grads, pieces, basis_out))
     grads = lax.all_gather(grads, "y", axis=0, tiled=True)
     basis_other = lax.ppermute(basis_out, "core", SWAP)
     middle = jnp.concatenate([basis_out[:, 256:], basis_other[:, :128]], axis=1)
     bases = jnp.stack([basis_out[:, :256], middle, basis_other[:, 128:]])
 
     acts = spread(pieces[:, :64], GRP, 8)
-    acts, bases = lax.optimization_barrier((acts, bases))
-    act = project_acts(acts, pieces)
-    own = act.reshape(8, 64, 256)
-    sums = exchange(own.astype(BF16), ("zh", "core")).astype(F32)
-    index = lax.axis_index(("zh", "core"))
-    mine = (jnp.arange(8) == index)[:, None, None]
-    act = jnp.sum(jnp.where(mine, own, sums), axis=0).astype(BF16)
-    act = spread(act, ("zh", "core"), 8).reshape(512, 256)
+    here, there = project_acts(core.astype(jnp.int32).reshape(1), acts, pieces)
+    own = here + lax.ppermute(there, "core", SWAP)
+    sums = spread(own.astype(BF16), "zh", 4)
+    sums, bases = lax.optimization_barrier((sums, bases))
+    mine = (jnp.arange(4) == lax.axis_index("zh"))[:, None, None]
+    act = jnp.sum(jnp.where(mine, own[None], sums.astype(F32)), axis=0).astype(BF16)
+    other = lax.ppermute(act, "core", SWAP)
+    act = jnp.concatenate([jnp.where(core == 0, act, other), jnp.where(core == 0, other, act)])
     partial = project_grads(grads, bases)
     _, partial = lax.optimization_barrier((act, partial))
     act = lax.all_gather(act, "y", axis=0)

time: 153 us -> 149 us (0.974)
  waiting for transfers between devices: 38.5 us -> 28.7 us
  Pallas kernels: 13.6 us -> 7.39 us
  local copies, waits for them, and re-layouts: 8.22 us -> 13.7 us
  starting transfers between devices: 37.8 us -> 42.2 us
  blocking collectives: 34.9 us -> 36.6 us
    all_to_all x5 -> x4, waiting for transfers between devices: 36.1 us -> 21.8 us  [exchange(): return lax.all_to_all(pieces, axis, 0, 0)]
    ppermute x0 -> x2, starting transfers between devices: none -> 9.45 us  [the longest x1 5.47 us: local(): own = here + lax.ppermute(there, 'core', SWAP)]
    pallas_call x2, Pallas kernels: 9.67 us -> 3.43 us  [the longest x1 3 us: project_grads(): pl.pallas_call(grad_kernel, in_specs=[VMEM, VMEM], out_specs=VMEM, out_sh...]
    unnamed x0 -> x4, local copies, waits for them, and re-layouts: none -> 4.59 us
    all_to_all x5 -> x4, starting transfers between devices: 32.7 us -> 28.1 us  [exchange(): return lax.all_to_all(pieces, axis, 0, 0)]
    all_gather x1, waiting for transfers between devices: 2.37 us -> 5.91 us  [local(): act = lax.all_gather(act, 'y', axis=0)]
    all_to_all x1, blocking collectives: 14.6 us -> 16.2 us  [exchange(): return lax.all_to_all(pieces, axis, 0, 0)]
  transfers between devices with their start and end apart: 8 -> 9, of which waited for: 5 -> 5; matrix products, arithmetic and copies ran while one was open for 9% -> 10% of each run, Pallas kernels for 6% -> 2%
where the time goes in v5:
time: 149 us; the launch traced here: 148 us
  starting transfers between devices  42.2 us (28%)
  blocking collectives  36.6 us (25%)
  waiting for transfers between devices  28.7 us (19%)
  local copies, waits for them, and re-layouts  13.7 us (9%)
  between operations  13.6 us (9%)
  Pallas kernels  7.39 us (5%)
  other arithmetic  5.84 us (4%)
    all_to_all x4, starting transfers between devices, exchange(): return lax.all_to_all(pieces, axis, 0, 0)  28.1 us
    all_to_all x4, waiting for transfers between devices, exchange(): return lax.all_to_all(pieces, axis, 0, 0)  21.8 us
    all_gather x1, blocking collectives, local(): grads = lax.all_gather(out_grads, 'zh', axis=0, tiled=True)  20.4 us
    all_to_all x1, blocking collectives, exchange(): return lax.all_to_all(pieces, axis, 0, 0)  16.2 us
    all_gather x1, waiting for transfers between devices, local(): act = lax.all_gather(act, 'y', axis=0)  5.91 us
    ppermute x1, starting transfers between devices, local(): own = here + lax.ppermute(there, 'core', SWAP)  5.47 us
    another operation x2, other arithmetic, local(): bases = jnp.stack([basis_out[:, :256], middle, basis_other[:, 128:]])  4.73 us
    unnamed x4, local copies, waits for them, and re-layouts  4.59 us
  transfers between devices with their start and end apart: 9, of which 5 were waited for; matrix products, arithmetic and copies ran while one was open for 10% of the time, Pallas kernels for 2%

profile of v5, /device:TPU:1, one launch (start us, length us, event | category | flops | bytes accessed | tf_op | source)
XLA Modules:
  0.0 147.9 jit_solution(5045909098088712227)
XLA Ops:
  6.5 2.1 %make_pieces.1 = bf16[8,320,128]{2,1,0:T(8,128)(2,1)} custom-call(s32[1]{0:T(128)} %bitcast.1.index_ref, bf16[1024,128]{1,0:T(8,128)(2,1)} %acts_ref.1, bf16[128,1024]{1,0:T(8,128)(2,1)} %weights_ref.1), custom_call_target="tpu_custom_call" | custom-call | tf_op jit(solution)/shard_map/make_pieces/pallas_call | solution.py:68
  8.7 7.7 %all-to-all-start = ((bf16[8,320,128]{2,1,0:T(8,128)(2,1)}), bf16[8,320,128]{2,1,0:T(8,128)(2,1)S(1)}, u32[]{:S(2)}, u32[]{:S(2)}) async-start(bf16[8,320,128]{2,1,0:T(8,128)(2,1)} %make_pieces.1), calls=%async_computation | async-start | bytes 1310720 | tf_op jit(solution)/shard_map/all_to_all | solution.py:25
  16.4 20.4 %all_gather.12 = bf16[64,3584]{1,0:T(8,128)(2,1)} all-gather(bf16[16,3584]{1,0:T(8,128)(2,1)} %param.4), channel_id=1, replica_groups=mesh['x'=4,'zl'=2,'y'=8,'zh'=4,'core'=2] {'zh'}, dimensions={0}, use_global_device_ids=true | all-gather | bytes 573440 | tf_op jit(solution)/shard_map/all_gather | solution.py:139
  36.8 1.2 broadcast_in_dim.23
  38.0 6.3 %all-to-all-start.1 = ((bf16[8,8,64,128]{3,2,1,0:T(8,128)(2,1)}), bf16[8,8,64,128]{3,2,1,0:T(8,128)(2,1)S(1)}, u32[]{:S(2)}, u32[]{:S(2)}) async-start(bf16[8,8,64,128]{3,2,1,0:T(8,128)(2,1)} %broadcast_in_dim.23), calls=%async_computation.1 | async-start | bytes 2097152 | tf_op jit(solution)/shard_map/all_to_all | solution.py:25
  44.3 4.5 %collective-permute-start.1 = (bf16[3584,384]{1,0:T(8,128)(2,1)}, bf16[3584,384]{1,0:T(8,128)(2,1)}, u32[]{:S(2)}, u32[]{:S(2)}) collective-permute-start(bf16[3584,384]{1,0:T(8,128)(2,1)} %param.6), channel_id=1, source_target_pairs={{0,1},{1,0},{2,3},{3,2},{4,5},{5,4},{6,7},{7,6},{8,9},{9,8},{10,11... | collective-permute-start | bytes 8257544 | tf_op jit(solution)/shard_map/ppermute | solution.py:142
  48.9 8.6 %all-to-all-done.1.acts_ref = bf16[8,8,64,128]{3,2,1,0:T(8,128)(2,1)S(1)} async-done(((bf16[8,8,64,128]{3,2,1,0:T(8,128)(2,1)}), bf16[8,8,64,128]{3,2,1,0:T(8,128)(2,1)S(1)}, u32[]{:S(2)}, u32[]{:S(2)}) %all-to-all-start.1) | async-done | bytes 1048608 | tf_op jit(solution)/shard_map/all_to_all | solution.py:25
  57.5 0.4 project_acts.1
  57.9 5.5 %collective-permute-start = (f32[256,256]{1,0:T(8,128)S(1)}, f32[256,256]{1,0:T(8,128)S(1)}, u32[]{:S(2)}, u32[]{:S(2)}) collective-permute-start(f32[256,256]{1,0:T(8,128)S(1)} %get-tuple-element.19), channel_id=1, source_target_pairs={{0,1},{1,0},{2,3},{3,2},{4,5},{5,4},{6,7},{7,6},{8,9},{9,8},{10,11... | collective-permute-start | bytes 786440 | tf_op jit(solution)/shard_map/ppermute | solution.py:148
  63.4 1.6 %slice_bitcast_fusion.1 = bf16[1,3584,256]{2,1,0:T(8,128)(2,1)S(1)} fusion(bf16[3584,384]{1,0:T(8,128)(2,1)} %param.6), kind=kLoop, calls=%fused_computation.3 | loop fusion | bytes 3670016 | tf_op jit(solution)/shard_map/stack | solution.py:144
  65.0 1.3 slice.23
  66.4 0.8 broadcast_in_dim.25
  67.2 9.1 %all-to-all-start.2 = ((bf16[4,256,256]{2,1,0:T(8,128)(2,1)}), bf16[4,256,256]{2,1,0:T(8,128)(2,1)S(1)}, u32[]{:S(2)}, u32[]{:S(2)}) async-start(bf16[4,256,256]{2,1,0:T(8,128)(2,1)} %broadcast_in_dim.25), calls=%async_computation.2 | async-start | bytes 1048576 | tf_op jit(solution)/shard_map/all_to_all | solution.py:25
  76.2 1.3 slice.28
  77.5 1.8 %slice_bitcast_fusion = (bf16[1,3584,256]{2,1,0:T(8,128)(2,1)S(1)}, bf16[1,3584,256]{2,1,0:T(8,128)(2,1)S(1)}) fusion(bf16[3584,384]{1,0:T(8,128)(2,1)} %collective-permute-done.1, bf16[3584,128]{1,0:T(8,128)(2,1)S(1)} %slice.28, bf16[3584,128]{1,0:T(8,128)(2,1)S(1)} %slice.23), kind=kLoop, calls=%fused_computation.1 | loop fusion | flops 3670016 | bytes 7340032 | tf_op jit(solution)/shard_map/stack | solution.py:144
  79.4 2.9 %pad_maximum_fusion.bases_ref = bf16[3,3584,256]{2,1,0:T(8,128)(2,1)} fusion(bf16[1,3584,256]{2,1,0:T(8,128)(2,1)S(1)} %get-tuple-element.31, bf16[1,3584,256]{2,1,0:T(8,128)(2,1)S(1)} %get-tuple-element.32, bf16[1,3584,256]{2,1,0:T(8,128)(2,1)S(1)} %slice_bitcast_fusion.1), kind=kLoop, calls=%fused_computation | loop fusion | flops 5505024 | bytes 11010048 | tf_op jit(solution)/shard_map/stack | solution.py:144
  82.2 7.9 %all-to-all-done.2 = bf16[4,256,256]{2,1,0:T(8,128)(2,1)S(1)} async-done(((bf16[4,256,256]{2,1,0:T(8,128)(2,1)}), bf16[4,256,256]{2,1,0:T(8,128)(2,1)S(1)}, u32[]{:S(2)}, u32[]{:S(2)}) %all-to-all-start.2) | async-done | bytes 524320 | tf_op jit(solution)/shard_map/all_to_all | solution.py:25
  90.2 0.2 select_reduce_fusion
  90.4 4.0 %collective-permute-start.2 = (bf16[256,256]{1,0:T(8,128)(2,1)S(1)}, bf16[256,256]{1,0:T(8,128)(2,1)S(1)}, u32[]{:S(2)}, u32[]{:S(2)}) collective-permute-start(bf16[256,256]{1,0:T(8,128)(2,1)S(1)} %select_reduce_fusion), channel_id=1, source_target_pairs={{0,1},{1,0},{2,3},{3,2},{4,5},{5,4},{6,7},{7,6},{8,9},{9,8},{10,11... | collective-permute-start | bytes 393224 | tf_op jit(solution)/shard_map/ppermute | solution.py:153
  94.3 1.0 collective-permute-done.2
  95.3 0.7 pad_maximum_fusion.1
  96.1 2.6 %copy-done = bf16[3,3584,256]{2,1,0:T(8,128)(2,1)S(1)} copy-done((bf16[3,3584,256]{2,1,0:T(8,128)(2,1)S(1)}, bf16[3,3584,256]{2,1,0:T(8,128)(2,1)}, u32[]{:S(2)}) %copy-start) | copy-done | bytes 5505048
  98.7 2.0 %copy-done.1 = bf16[512,3584]{1,0:T(8,128)(2,1)S(1)} copy-done((bf16[512,3584]{1,0:T(8,128)(2,1)S(1)}, bf16[512,3584]{1,0:T(8,128)(2,1)}, u32[]{:S(2)}) %copy-start.1) | copy-done | bytes 3670040
  100.7 3.0 %project_grads.1 = bf16[512,768]{1,0:T(8,128)(2,1)S(1)} custom-call(bf16[512,3584]{1,0:T(8,128)(2,1)S(1)} %copy-done.1, bf16[3,3584,256]{2,1,0:T(8,128)(2,1)S(1)} %copy-done), custom_call_target="tpu_custom_call" | custom-call | tf_op jit(solution)/shard_map/project_grads/pallas_call | solution.py:42
  103.7 16.2 %all_to_all.25 = bf16[8,64,768]{2,1,0:T(8,128)(2,1)S(1)} all-to-all(bf16[8,64,768]{2,1,0:T(8,128)(2,1)S(1)} %bitcast.20), channel_id=1, replica_groups=mesh['x'=4,'zl'=2,'y'=8,'zh'=4,'core'=2] {'x','zl'}, dimensions={0} | all-to-all | bytes 1572864 | tf_op jit(solution)/shard_map/all_to_all | solution.py:25
  119.9 0.1 reduce_sum.22
  120.1 1.0 broadcast_in_dim.40
  121.0 5.2 %all-to-all-start.4 = ((bf16[16,64,384]{2,1,0:T(8,128)(2,1)}), bf16[16,64,384]{2,1,0:T(8,128)(2,1)S(1)}, u32[]{:S(2)}, u32[]{:S(2)}) async-start(bf16[16,64,384]{2,1,0:T(8,128)(2,1)} %bitcast.8), calls=%async_computation.4 | async-start | bytes 1572864 | tf_op jit(solution)/shard_map/all_to_all | solution.py:25
  126.2 5.9 %all-gather.6.cloned.1.call-done = bf16[4096,256]{1,0:T(8,128)(2,1)} async-done(((bf16[512,256]{1,0:T(8,128)(2,1)}), bf16[4096,256]{1,0:T(8,128)(2,1)}) %all-gather.6.cloned.1.call-update) | async-done | bytes 2097168 | tf_op jit(solution)/shard_map/all_gather | solution.py:157
  132.1 1.9 %copy.6 = bf16[8,4,2,4,16,256]{5,4,3,2,1,0:T(8,128)(2,1)S(1)} copy(bf16[8,4,2,4,16,256]{5,4,2,3,1,0:T(8,128)(2,1)} %bitcast.22) | data formatting | bytes 4194304 | tf_op jit(solution)/shard_map/transpose | solution.py:158
  134.0 5.3 %all-to-all-done.4 = bf16[16,64,384]{2,1,0:T(8,128)(2,1)S(1)} async-done(((bf16[16,64,384]{2,1,0:T(8,128)(2,1)}), bf16[16,64,384]{2,1,0:T(8,128)(2,1)S(1)}, u32[]{:S(2)}, u32[]{:S(2)}) %all-to-all-start.4) | async-done | bytes 786464 | tf_op jit(solution)/shard_map/all_to_all | solution.py:25
  139.3 1.8 %fit_blocks.1 = f32[384,1024]{1,0:T(8,128)} custom-call(bf16[1024,384]{1,0:T(8,128)(2,1)S(1)} %bitcast.21, bf16[8,512,256]{2,1,0:T(8,128)(2,1)S(1)} %bitcast.19), custom_call_target="tpu_custom_call" | custom-call | tf_op jit(solution)/shard_map/fit_blocks/pallas_call | solution.py:120
  (16 shorter events, 0.2 us)
Async XLA Ops:
  8.7 28.1 %all-to-all-start = ((bf16[8,320,128]{2,1,0:T(8,128)(2,1)}), bf16[8,320,128]{2,1,0:T(8,128)(2,1)S(1)}, u32[]{:S(2)}, u32[]{:S(2)}) async-start(bf16[8,320,128]{2,1,0:T(8,128)(2,1)} %make_pieces.1), calls=%async_computation | async-start | bytes 1310720 | tf_op jit(solution)/shard_map/all_to_all | solution.py:25
  16.4 79.7 %all-gather.4.cloned.1.call-start = ((), (), s32[]{:S(2)}) async-start(), calls=%async_computation.5 | async-start | bytes 4128768 | tf_op jit(solution)/shard_map/all_gather | solution.py:141
  38.0 19.5 %all-to-all-start.1 = ((bf16[8,8,64,128]{3,2,1,0:T(8,128)(2,1)}), bf16[8,8,64,128]{3,2,1,0:T(8,128)(2,1)S(1)}, u32[]{:S(2)}, u32[]{:S(2)}) async-start(bf16[8,8,64,128]{3,2,1,0:T(8,128)(2,1)} %broadcast_in_dim.23), calls=%async_computation.1 | async-start | bytes 2097152 | tf_op jit(solution)/shard_map/all_to_all | solution.py:25
  44.3 31.9 %collective-permute-start.1 = (bf16[3584,384]{1,0:T(8,128)(2,1)}, bf16[3584,384]{1,0:T(8,128)(2,1)}, u32[]{:S(2)}, u32[]{:S(2)}) collective-permute-start(bf16[3584,384]{1,0:T(8,128)(2,1)} %param.6), channel_id=1, source_target_pairs={{0,1},{1,0},{2,3},{3,2},{4,5},{5,4},{6,7},{7,6},{8,9},{9,8},{10,11... | collective-permute-start | bytes 8257544 | tf_op jit(solution)/shard_map/ppermute | solution.py:142
  57.9 8.4 %collective-permute-start = (f32[256,256]{1,0:T(8,128)S(1)}, f32[256,256]{1,0:T(8,128)S(1)}, u32[]{:S(2)}, u32[]{:S(2)}) collective-permute-start(f32[256,256]{1,0:T(8,128)S(1)} %get-tuple-element.19), channel_id=1, source_target_pairs={{0,1},{1,0},{2,3},{3,2},{4,5},{5,4},{6,7},{7,6},{8,9},{9,8},{10,11... | collective-permute-start | bytes 786440 | tf_op jit(solution)/shard_map/ppermute | solution.py:148
  67.2 23.0 %all-to-all-start.2 = ((bf16[4,256,256]{2,1,0:T(8,128)(2,1)}), bf16[4,256,256]{2,1,0:T(8,128)(2,1)S(1)}, u32[]{:S(2)}, u32[]{:S(2)}) async-start(bf16[4,256,256]{2,1,0:T(8,128)(2,1)} %broadcast_in_dim.25), calls=%async_computation.2 | async-start | bytes 1048576 | tf_op jit(solution)/shard_map/all_to_all | solution.py:25
  76.2 55.9 %all-gather.6.cloned.1.call-start = ((), (), s32[]{:S(2)}) async-start(), calls=%async_computation.6 | async-start | bytes 2359296 | tf_op jit(solution)/shard_map/all_gather | solution.py:157
  90.4 5.0 %collective-permute-start.2 = (bf16[256,256]{1,0:T(8,128)(2,1)S(1)}, bf16[256,256]{1,0:T(8,128)(2,1)S(1)}, u32[]{:S(2)}, u32[]{:S(2)}) collective-permute-start(bf16[256,256]{1,0:T(8,128)(2,1)S(1)} %select_reduce_fusion), channel_id=1, source_target_pairs={{0,1},{1,0},{2,3},{3,2},{4,5},{5,4},{6,7},{7,6},{8,9},{9,8},{10,11... | collective-permute-start | bytes 393224 | tf_op jit(solution)/shard_map/ppermute | solution.py:153
  96.1 2.6 %copy-start = (bf16[3,3584,256]{2,1,0:T(8,128)(2,1)S(1)}, bf16[3,3584,256]{2,1,0:T(8,128)(2,1)}, u32[]{:S(2)}) copy-start(bf16[3,3584,256]{2,1,0:T(8,128)(2,1)} %pad_maximum_fusion.bases_ref) | copy-start | bytes 16515076
  98.7 2.0 %copy-start.1 = (bf16[512,3584]{1,0:T(8,128)(2,1)S(1)}, bf16[512,3584]{1,0:T(8,128)(2,1)}, u32[]{:S(2)}) copy-start(bf16[512,3584]{1,0:T(8,128)(2,1)} %all-gather.4.cloned.1.call-done.grads_ref) | copy-start | bytes 11010052
  121.0 18.2 %all-to-all-start.4 = ((bf16[16,64,384]{2,1,0:T(8,128)(2,1)}), bf16[16,64,384]{2,1,0:T(8,128)(2,1)S(1)}, u32[]{:S(2)}, u32[]{:S(2)}) async-start(bf16[16,64,384]{2,1,0:T(8,128)(2,1)} %bitcast.8), calls=%async_computation.4 | async-start | bytes 1572864 | tf_op jit(solution)/shard_map/all_to_all | solution.py:25
Sparse Core Ops, SparseCore 0:
  36.9 54.0 all-gather.3
  96.2 35.8 all-gather.5

commit v6 on v5

--- a/solution.py
+++ b/solution.py
@@ -47,6 +47,24 @@
         compiler_params=PARAMS,
         name="project_grads",
     )(grads, bases)
+
+
+def join_kernel(mine_ref, other_ref, out_ref):
+    out_ref[0] = mine_ref[:, :256]
+    out_ref[1, :, :128] = mine_ref[:, 256:]
+    out_ref[1, :, 128:] = other_ref[:, :128]
+    out_ref[2] = other_ref[:, 128:]
+
+
+def join(mine, other):
+    return pl.pallas_call(
+        join_kernel,
+        in_specs=[VMEM, VMEM],
+        out_specs=VMEM,
+        out_shape=jax.ShapeDtypeStruct((3, 3584, 256), BF16),
+        compiler_params=PARAMS,
+        name="join_bases",
+    )(mine, other)
 
 
 def pieces_kernel(index_ref, acts_ref, weights_ref, out_ref, sems):
@@ -140,8 +158,7 @@
     grads, pieces, basis_out = lax.optimization_barrier((grads, pieces, basis_out))
     grads = lax.all_gather(grads, "y", axis=0, tiled=True)
     basis_other = lax.ppermute(basis_out, "core", SWAP)
-    middle = jnp.concatenate([basis_out[:, 256:], basis_other[:, :128]], axis=1)
-    bases = jnp.stack([basis_out[:, :256], middle, basis_other[:, 128:]])
+    bases = join(basis_out, basis_other)
 
     acts = spread(pieces[:, :64], GRP, 8)
     here, there = project_acts(core.astype(jnp.int32).reshape(1), acts, pieces)

time: 149 us -> 147 us (0.987)
  other arithmetic: 5.84 us -> 1.1 us
  Pallas kernels: 7.39 us -> 9.74 us
    another operation x2 -> x0, other arithmetic: 4.73 us -> none  [local(): bases = jnp.stack([basis_out[:, :256], middle, basis_other[:, 128:]])]
    unnamed x4 -> x8, local copies, waits for them, and re-layouts: 4.59 us -> 8.8 us
    all_to_all x4, waiting for transfers between devices: 21.8 us -> 19.3 us  [exchange(): return lax.all_to_all(pieces, axis, 0, 0)]
    slice x2 -> x0, local copies, waits for them, and re-layouts: 2.52 us -> none  [local(): middle = jnp.concatenate([basis_out[:, 256:], basis_other[:, :128]], axis=1)]
    pallas_call x0 -> x1, Pallas kernels: none -> 2.35 us  [join(): pl.pallas_call(join_kernel, in_specs=[VMEM, VMEM], out_specs=VMEM, out_sh...]
    all_gather x1, waiting for transfers between devices: 5.91 us -> 7.7 us  [local(): act = lax.all_gather(act, 'y', axis=0)]
    another operation x1 -> x0, local copies, waits for them, and re-layouts: 1.63 us -> none  [local(): bases = jnp.stack([basis_out[:, :256], middle, basis_other[:, 128:]])]
  transfers between devices with their start and end apart: 9 -> 9, of which waited for: 5 -> 6; matrix products, arithmetic and copies ran while one was open for 10% -> 4% of each run, Pallas kernels for 2% -> 4%
where the time goes in v6:
time: 147 us; the launch traced here: 146 us
  starting transfers between devices  42.4 us (29%)
  blocking collectives  36.4 us (25%)
  waiting for transfers between devices  29.1 us (20%)
  local copies, waits for them, and re-layouts  13.7 us (9%)
  between operations  13.6 us (9%)
  Pallas kernels  9.74 us (7%)
    all_to_all x4, starting transfers between devices, exchange(): return lax.all_to_all(pieces, axis, 0, 0)  28.2 us
    all_gather x1, blocking collectives, local(): grads = lax.all_gather(out_grads, 'zh', axis=0, tiled=True)  20.4 us
    all_to_all x4, waiting for transfers between devices, exchange(): return lax.all_to_all(pieces, axis, 0, 0)  19.3 us
    all_to_all x1, blocking collectives, exchange(): return lax.all_to_all(pieces, axis, 0, 0)  16.1 us
    unnamed x8, local copies, waits for them, and re-layouts  8.8 us
    all_gather x1, waiting for transfers between devices, local(): act = lax.all_gather(act, 'y', axis=0)  7.7 us
    ppermute x1, starting transfers between devices, local(): own = here + lax.ppermute(there, 'core', SWAP)  5.47 us
    ppermute x1, starting transfers between devices, local(): basis_other = lax.ppermute(basis_out, 'core', SWAP)  4.54 us
  transfers between devices with their start and end apart: 9, of which 6 were waited for; matrix products, arithmetic and copies ran while one was open for 4% of the time, Pallas kernels for 4%

profile of v6, /device:TPU:1, one launch (start us, length us, event | category | flops | bytes accessed | tf_op | source)
XLA Modules:
  0.0 146.1 jit_solution(11675753795356624481)
XLA Ops:
  6.5 2.1 %make_pieces.1 = bf16[8,320,128]{2,1,0:T(8,128)(2,1)} custom-call(s32[1]{0:T(128)} %bitcast.1.index_ref, bf16[1024,128]{1,0:T(8,128)(2,1)} %acts_ref.1, bf16[128,1024]{1,0:T(8,128)(2,1)} %weights_ref.1), custom_call_target="tpu_custom_call" | custom-call | tf_op jit(solution)/shard_map/make_pieces/pallas_call | solution.py:86
  8.7 7.7 %all-to-all-start = ((bf16[8,320,128]{2,1,0:T(8,128)(2,1)}), bf16[8,320,128]{2,1,0:T(8,128)(2,1)S(1)}, u32[]{:S(2)}, u32[]{:S(2)}) async-start(bf16[8,320,128]{2,1,0:T(8,128)(2,1)} %make_pieces.1), calls=%async_computation | async-start | bytes 1310720 | tf_op jit(solution)/shard_map/all_to_all | solution.py:25
  16.4 0.0 all-gather.4.cloned.1.call-start
  16.4 20.4 %all_gather.12 = bf16[64,3584]{1,0:T(8,128)(2,1)} all-gather(bf16[16,3584]{1,0:T(8,128)(2,1)} %param.4), channel_id=1, replica_groups=mesh['x'=4,'zl'=2,'y'=8,'zh'=4,'core'=2] {'zh'}, dimensions={0}, use_global_device_ids=true | all-gather | bytes 573440 | tf_op jit(solution)/shard_map/all_gather | solution.py:157
  36.8 1.2 broadcast_in_dim.23
  38.0 6.3 %all-to-all-start.1 = ((bf16[8,8,64,128]{3,2,1,0:T(8,128)(2,1)}), bf16[8,8,64,128]{3,2,1,0:T(8,128)(2,1)S(1)}, u32[]{:S(2)}, u32[]{:S(2)}) async-start(bf16[8,8,64,128]{3,2,1,0:T(8,128)(2,1)} %broadcast_in_dim.23), calls=%async_computation.1 | async-start | bytes 2097152 | tf_op jit(solution)/shard_map/all_to_all | solution.py:25
  44.3 4.5 %collective-permute-start.1 = (bf16[3584,384]{1,0:T(8,128)(2,1)}, bf16[3584,384]{1,0:T(8,128)(2,1)}, u32[]{:S(2)}, u32[]{:S(2)}) collective-permute-start(bf16[3584,384]{1,0:T(8,128)(2,1)} %mine_ref), channel_id=1, source_target_pairs={{0,1},{1,0},{2,3},{3,2},{4,5},{5,4},{6,7},{7,6},{8,9},{9,8},{10,11... | collective-permute-start | bytes 8257544 | tf_op jit(solution)/shard_map/ppermute | solution.py:160
  48.9 8.6 %all-to-all-done.1.acts_ref = bf16[8,8,64,128]{3,2,1,0:T(8,128)(2,1)S(1)} async-done(((bf16[8,8,64,128]{3,2,1,0:T(8,128)(2,1)}), bf16[8,8,64,128]{3,2,1,0:T(8,128)(2,1)S(1)}, u32[]{:S(2)}, u32[]{:S(2)}) %all-to-all-start.1) | async-done | bytes 1048608 | tf_op jit(solution)/shard_map/all_to_all | solution.py:25
  57.5 0.4 project_acts.1
  57.9 5.5 %collective-permute-start = (f32[256,256]{1,0:T(8,128)S(1)}, f32[256,256]{1,0:T(8,128)S(1)}, u32[]{:S(2)}, u32[]{:S(2)}) collective-permute-start(f32[256,256]{1,0:T(8,128)S(1)} %get-tuple-element.19), channel_id=1, source_target_pairs={{0,1},{1,0},{2,3},{3,2},{4,5},{5,4},{6,7},{7,6},{8,9},{9,8},{10,11... | collective-permute-start | bytes 786440 | tf_op jit(solution)/shard_map/ppermute | solution.py:165
  63.4 1.1 collective-permute-done
  64.6 0.8 broadcast_in_dim.25
  65.4 9.1 %all-to-all-start.2 = ((bf16[4,256,256]{2,1,0:T(8,128)(2,1)}), bf16[4,256,256]{2,1,0:T(8,128)(2,1)S(1)}, u32[]{:S(2)}, u32[]{:S(2)}) async-start(bf16[4,256,256]{2,1,0:T(8,128)(2,1)} %broadcast_in_dim.25), calls=%async_computation.2 | async-start | bytes 1048576 | tf_op jit(solution)/shard_map/all_to_all | solution.py:25
  74.5 1.8 %copy-done.3 = bf16[3584,384]{1,0:T(8,128)(2,1)S(1)} copy-done((bf16[3584,384]{1,0:T(8,128)(2,1)S(1)}, bf16[3584,384]{1,0:T(8,128)(2,1)}, u32[]{:S(2)}) %copy-start.3) | copy-done | bytes 2752536
  76.3 2.4 %join_bases.1.bases_ref = bf16[3,3584,256]{2,1,0:T(8,128)(2,1)S(1)} custom-call(bf16[3584,384]{1,0:T(8,128)(2,1)S(1)} %copy-done.3, bf16[3584,384]{1,0:T(8,128)(2,1)} %collective-permute-done.1.other_ref), custom_call_target="tpu_custom_call" | custom-call | tf_op jit(solution)/shard_map/join_bases/pallas_call | solution.py:60
  78.7 2.4 %copy-done = bf16[3,3584,256]{2,1,0:T(8,128)(2,1)} copy-done((bf16[3,3584,256]{2,1,0:T(8,128)(2,1)}, bf16[3,3584,256]{2,1,0:T(8,128)(2,1)S(1)}, u32[]{:S(2)}) %copy-start) | copy-done | bytes 5505048
  81.1 7.2 %all-to-all-done.2 = bf16[4,256,256]{2,1,0:T(8,128)(2,1)S(1)} async-done(((bf16[4,256,256]{2,1,0:T(8,128)(2,1)}), bf16[4,256,256]{2,1,0:T(8,128)(2,1)S(1)}, u32[]{:S(2)}, u32[]{:S(2)}) %all-to-all-start.2) | async-done | bytes 524320 | tf_op jit(solution)/shard_map/all_to_all | solution.py:25
  88.3 0.2 select_reduce_fusion
  88.4 4.2 %collective-permute-start.2 = (bf16[256,256]{1,0:T(8,128)(2,1)S(1)}, bf16[256,256]{1,0:T(8,128)(2,1)S(1)}, u32[]{:S(2)}, u32[]{:S(2)}) collective-permute-start(bf16[256,256]{1,0:T(8,128)(2,1)S(1)} %select_reduce_fusion), channel_id=1, source_target_pairs={{0,1},{1,0},{2,3},{3,2},{4,5},{5,4},{6,7},{7,6},{8,9},{9,8},{10,11... | collective-permute-start | bytes 393224 | tf_op jit(solution)/shard_map/ppermute | solution.py:170
  92.7 1.0 collective-permute-done.2
  93.7 0.7 pad_maximum_fusion
  94.4 2.6 %copy-done.1 = bf16[3,3584,256]{2,1,0:T(8,128)(2,1)S(1)} copy-done((bf16[3,3584,256]{2,1,0:T(8,128)(2,1)S(1)}, bf16[3,3584,256]{2,1,0:T(8,128)(2,1)}, u32[]{:S(2)}) %copy-start.1) | copy-done | bytes 5505048
  97.0 2.0 %copy-done.2 = bf16[512,3584]{1,0:T(8,128)(2,1)S(1)} copy-done((bf16[512,3584]{1,0:T(8,128)(2,1)S(1)}, bf16[512,3584]{1,0:T(8,128)(2,1)}, u32[]{:S(2)}) %copy-start.2) | copy-done | bytes 3670040
  99.0 3.0 %project_grads.1 = bf16[512,768]{1,0:T(8,128)(2,1)S(1)} custom-call(bf16[512,3584]{1,0:T(8,128)(2,1)S(1)} %copy-done.2, bf16[3,3584,256]{2,1,0:T(8,128)(2,1)S(1)} %copy-done.1), custom_call_target="tpu_custom_call" | custom-call | tf_op jit(solution)/shard_map/project_grads/pallas_call | solution.py:42
  102.0 16.1 %all_to_all.25 = bf16[8,64,768]{2,1,0:T(8,128)(2,1)S(1)} all-to-all(bf16[8,64,768]{2,1,0:T(8,128)(2,1)S(1)} %bitcast.14), channel_id=1, replica_groups=mesh['x'=4,'zl'=2,'y'=8,'zh'=4,'core'=2] {'x','zl'}, dimensions={0} | all-to-all | bytes 1572864 | tf_op jit(solution)/shard_map/all_to_all | solution.py:25
  118.1 0.1 reduce_sum.22
  118.3 1.0 broadcast_in_dim.40
  119.2 5.2 %all-to-all-start.4 = ((bf16[16,64,384]{2,1,0:T(8,128)(2,1)}), bf16[16,64,384]{2,1,0:T(8,128)(2,1)S(1)}, u32[]{:S(2)}, u32[]{:S(2)}) async-start(bf16[16,64,384]{2,1,0:T(8,128)(2,1)} %bitcast.5), calls=%async_computation.4 | async-start | bytes 1572864 | tf_op jit(solution)/shard_map/all_to_all | solution.py:25
  124.4 7.7 %all-gather.6.cloned.1.call-done = bf16[4096,256]{1,0:T(8,128)(2,1)} async-done(((bf16[512,256]{1,0:T(8,128)(2,1)}), bf16[4096,256]{1,0:T(8,128)(2,1)}) %all-gather.6.cloned.1.call-update) | async-done | bytes 2097168 | tf_op jit(solution)/shard_map/all_gather | solution.py:174
  132.1 1.9 %copy.6 = bf16[8,4,2,4,16,256]{5,4,3,2,1,0:T(8,128)(2,1)S(1)} copy(bf16[8,4,2,4,16,256]{5,4,2,3,1,0:T(8,128)(2,1)} %bitcast.16) | data formatting | bytes 4194304 | tf_op jit(solution)/shard_map/transpose | solution.py:175
  134.0 3.5 %all-to-all-done.4 = bf16[16,64,384]{2,1,0:T(8,128)(2,1)S(1)} async-done(((bf16[16,64,384]{2,1,0:T(8,128)(2,1)}), bf16[16,64,384]{2,1,0:T(8,128)(2,1)S(1)}, u32[]{:S(2)}, u32[]{:S(2)}) %all-to-all-start.4) | async-done | bytes 786464 | tf_op jit(solution)/shard_map/all_to_all | solution.py:25
  137.5 1.8 %fit_blocks.1 = f32[384,1024]{1,0:T(8,128)} custom-call(bf16[1024,384]{1,0:T(8,128)(2,1)S(1)} %bitcast.15, bf16[8,512,256]{2,1,0:T(8,128)(2,1)S(1)} %bitcast.13), custom_call_target="tpu_custom_call" | custom-call | tf_op jit(solution)/shard_map/fit_blocks/pallas_call | solution.py:138
  (16 shorter events, 0.2 us)
Async XLA Ops:
  8.7 28.1 %all-to-all-start = ((bf16[8,320,128]{2,1,0:T(8,128)(2,1)}), bf16[8,320,128]{2,1,0:T(8,128)(2,1)S(1)}, u32[]{:S(2)}, u32[]{:S(2)}) async-start(bf16[8,320,128]{2,1,0:T(8,128)(2,1)} %make_pieces.1), calls=%async_computation | async-start | bytes 1310720 | tf_op jit(solution)/shard_map/all_to_all | solution.py:25
  16.4 78.1 %all-gather.4.cloned.1.call-start = ((), (), s32[]{:S(2)}) async-start(), calls=%async_computation.5 | async-start | bytes 4128768 | tf_op jit(solution)/shard_map/all_gather | solution.py:159
  38.0 19.5 %all-to-all-start.1 = ((bf16[8,8,64,128]{3,2,1,0:T(8,128)(2,1)}), bf16[8,8,64,128]{3,2,1,0:T(8,128)(2,1)S(1)}, u32[]{:S(2)}, u32[]{:S(2)}) async-start(bf16[8,8,64,128]{3,2,1,0:T(8,128)(2,1)} %broadcast_in_dim.23), calls=%async_computation.1 | async-start | bytes 2097152 | tf_op jit(solution)/shard_map/all_to_all | solution.py:25
  44.3 30.2 %collective-permute-start.1 = (bf16[3584,384]{1,0:T(8,128)(2,1)}, bf16[3584,384]{1,0:T(8,128)(2,1)}, u32[]{:S(2)}, u32[]{:S(2)}) collective-permute-start(bf16[3584,384]{1,0:T(8,128)(2,1)} %mine_ref), channel_id=1, source_target_pairs={{0,1},{1,0},{2,3},{3,2},{4,5},{5,4},{6,7},{7,6},{8,9},{9,8},{10,11... | collective-permute-start | bytes 8257544 | tf_op jit(solution)/shard_map/ppermute | solution.py:160
  57.9 6.6 %collective-permute-start = (f32[256,256]{1,0:T(8,128)S(1)}, f32[256,256]{1,0:T(8,128)S(1)}, u32[]{:S(2)}, u32[]{:S(2)}) collective-permute-start(f32[256,256]{1,0:T(8,128)S(1)} %get-tuple-element.19), channel_id=1, source_target_pairs={{0,1},{1,0},{2,3},{3,2},{4,5},{5,4},{6,7},{7,6},{8,9},{9,8},{10,11... | collective-permute-start | bytes 786440 | tf_op jit(solution)/shard_map/ppermute | solution.py:165
  65.4 22.8 %all-to-all-start.2 = ((bf16[4,256,256]{2,1,0:T(8,128)(2,1)}), bf16[4,256,256]{2,1,0:T(8,128)(2,1)S(1)}, u32[]{:S(2)}, u32[]{:S(2)}) async-start(bf16[4,256,256]{2,1,0:T(8,128)(2,1)} %broadcast_in_dim.25), calls=%async_computation.2 | async-start | bytes 1048576 | tf_op jit(solution)/shard_map/all_to_all | solution.py:25
  74.5 57.6 %all-gather.6.cloned.1.call-start = ((), (), s32[]{:S(2)}) async-start(), calls=%async_computation.6 | async-start | bytes 2359296 | tf_op jit(solution)/shard_map/all_gather | solution.py:174
  74.5 1.8 %copy-start.3 = (bf16[3584,384]{1,0:T(8,128)(2,1)S(1)}, bf16[3584,384]{1,0:T(8,128)(2,1)}, u32[]{:S(2)}) copy-start(bf16[3584,384]{1,0:T(8,128)(2,1)} %mine_ref) | copy-start | bytes 8257540
  78.7 2.4 %copy-start = (bf16[3,3584,256]{2,1,0:T(8,128)(2,1)}, bf16[3,3584,256]{2,1,0:T(8,128)(2,1)S(1)}, u32[]{:S(2)}) copy-start(bf16[3,3584,256]{2,1,0:T(8,128)(2,1)S(1)} %join_bases.1.bases_ref) | copy-start | bytes 16515076
  88.4 5.2 %collective-permute-start.2 = (bf16[256,256]{1,0:T(8,128)(2,1)S(1)}, bf16[256,256]{1,0:T(8,128)(2,1)S(1)}, u32[]{:S(2)}, u32[]{:S(2)}) collective-permute-start(bf16[256,256]{1,0:T(8,128)(2,1)S(1)} %select_reduce_fusion), channel_id=1, source_target_pairs={{0,1},{1,0},{2,3},{3,2},{4,5},{5,4},{6,7},{7,6},{8,9},{9,8},{10,11... | collective-permute-start | bytes 393224 | tf_op jit(solution)/shard_map/ppermute | solution.py:170
  94.4 2.6 %copy-start.1 = (bf16[3,3584,256]{2,1,0:T(8,128)(2,1)S(1)}, bf16[3,3584,256]{2,1,0:T(8,128)(2,1)}, u32[]{:S(2)}) copy-start(bf16[3,3584,256]{2,1,0:T(8,128)(2,1)} %copy-done) | copy-start | bytes 16515076
  97.0 2.0 %copy-start.2 = (bf16[512,3584]{1,0:T(8,128)(2,1)S(1)}, bf16[512,3584]{1,0:T(8,128)(2,1)}, u32[]{:S(2)}) copy-start(bf16[512,3584]{1,0:T(8,128)(2,1)} %all-gather.4.cloned.1.call-done.grads_ref) | copy-start | bytes 11010052
  119.2 18.2 %all-to-all-start.4 = ((bf16[16,64,384]{2,1,0:T(8,128)(2,1)}), bf16[16,64,384]{2,1,0:T(8,128)(2,1)S(1)}, u32[]{:S(2)}, u32[]{:S(2)}) async-start(bf16[16,64,384]{2,1,0:T(8,128)(2,1)} %bitcast.5), calls=%async_computation.4 | async-start | bytes 1572864 | tf_op jit(solution)/shard_map/all_to_all | solution.py:25
Sparse Core Ops, SparseCore 0:
  36.9 54.0 all-gather.3
  94.5 37.5 all-gather.5
